TPU v7x, 512 devices: a whole 4x4x16 slice. The times are simulated.
512 devices in a mesh: blk: 32 (over x, z_lo), grp: 16 (over z_hi, y, core).
Axes of the slice: x: 4, y: 4, z: 16 (z_hi: 2, z_lo: 8; z = z_hi * 8 + z_lo), core: 2. Of those that a mesh axis runs over, the one named last changes fastest.
Arguments:
- amplitudes: bfloat16 [128, 2048, 2048], P(None, 'blk', 'grp'), may hold values from -6 to 6
- amplitude_map: int32 [32, 32], P('blk', 'grp'), may hold values 0 or 1
- integrals: bfloat16 [2048, 2048], P('blk'), may hold values from -0.375 to 0.375
- integral_map: int32 [32, 32], P('blk'), may hold values from 0 to 1, as said below
- pair_list: int32 [128, 2], replicated, may hold values from 0 to 127
- occupied_energy: float32 [128], replicated, may hold values from -3 to -0.3
- virtual_energy: float32 [2048], replicated, may hold values from 0.2 to 3
Outputs:
- update: bfloat16 [128, 2048, 2048], P(None, 'blk', 'grp')
Inputs may be any that keep to these rules, and one draw needn't show every extreme that they name: `integral_map`: each tile row holds between 2 and 16 nonzero tiles, its diagonal tile among them; some tile row holds exactly 16.
All inputs are finite; a program needn't handle non-finite values. No bound on the sum of `amplitude_map` on one device may be relied on, other than what follows from the above.
Results may differ from a plain program's by a relative error of at most 0.0049.
Values may be sent and summed in bfloat16 or wider, within the bound.
A program may use at most 128 MiB of HBM per device.

v0:
```python
import jax
import jax.numpy as jnp
from jax import lax
from jax.sharding import PartitionSpec as P

TILE = 64


def body(
    amplitudes, amplitude_map, integrals, integral_map, pair_list, occupied_energy, virtual_energy
):
    amp_mask = jnp.repeat(jnp.repeat(amplitude_map, TILE, axis=0), TILE, axis=1).astype(
        jnp.bfloat16
    )
    masked_amp = amplitudes * amp_mask[None]
    row_view = lax.all_to_all(masked_amp, "grp", split_axis=1, concat_axis=2, tiled=True)
    pair_count, sub_rows, width = row_view.shape
    flat_rows = row_view.reshape(pair_count * sub_rows, width)
    int_mask = jnp.repeat(jnp.repeat(integral_map, TILE, axis=0), TILE, axis=1).astype(jnp.bfloat16)
    masked_int = integrals * int_mask
    product = lax.dot_general(
        flat_rows,
        lax.all_gather(masked_int, "blk", axis=0, tiled=True),
        (((1,), (1,)), ((), ())),
        preferred_element_type=jnp.float32,
    )
    ladder = product.reshape(pair_count, sub_rows, width).astype(jnp.bfloat16)
    column_view = lax.all_to_all(ladder, "grp", split_axis=2, concat_axis=1, tiled=True)
    local_rows = column_view.shape[1]
    local_cols = column_view.shape[2]
    row_start = lax.axis_index("blk") * local_rows
    col_start = lax.axis_index("grp") * local_cols
    energy_rows = lax.dynamic_slice_in_dim(virtual_energy, row_start, local_rows, 0)
    energy_cols = lax.dynamic_slice_in_dim(virtual_energy, col_start, local_cols, 0)
    occupied_ids = jnp.arange(occupied_energy.shape[0], dtype=jnp.int32)
    first_hot = (pair_list[:, 0:1] == occupied_ids[None, :]).astype(jnp.float32)
    second_hot = (pair_list[:, 1:2] == occupied_ids[None, :]).astype(jnp.float32)
    shifts = jnp.sum((first_hot + second_hot) * occupied_energy[None, :], axis=1)
    denominator = energy_rows[None, :, None] + energy_cols[None, None, :] - shifts[:, None, None]
    return (column_view.astype(jnp.float32) / denominator).astype(jnp.bfloat16)


def solution(mesh):
    in_specs = (
        P(None, "blk", "grp"),
        P("blk", "grp"),
        P("blk", None),
        P("blk", None),
        P(),
        P(),
        P(),
    )
    out_specs = P(None, "blk", "grp")
    return jax.shard_map(body, mesh=mesh, in_specs=in_specs, out_specs=out_specs, check_vma=False)
```

profile of v0, /device:TPU:121, one launch (start us, length us, event | category | flops | bytes accessed | tf_op | source)
XLA Modules:
  0.0 475.2 jit_solution(3242384022899630897)
XLA Ops:
  6.5 0.0 all-gather.2.cloned.1.call-start
  6.5 0.7 convert_bitcast_fusion.1
  7.2 0.1 broadcast_in_dim.7
  7.3 0.1 convert_element_type.52
  7.4 1.7 broadcast_multiply_fusion
  9.1 0.0 all-gather.2.cloned.1.call-update
  9.1 0.7 convert_bitcast_fusion.2
  9.7 0.1 broadcast_in_dim.6
  9.8 0.1 convert_element_type.49
  9.9 3.3 copy_multiply_fusion
  13.2 161.9 %all_to_all.24 = bf16[128,64,128]{2,0,1:T(8,128)(2,1)S(1)} all-to-all(bf16[128,64,128]{2,0,1:T(8,128)(2,1)S(1)} %copy_multiply_fusion), channel_id=1, replica_groups=mesh['blk'=32,'grp'=16] {'grp'}, dimensions={1} | all-to-all | bytes 4194304 | tf_op jit(solution)/shard_map/all_to_all | solution.py:16
  175.2 1.4 copy.20
  176.5 2.3 dot_general.5
  178.8 136.5 %all-gather.2.cloned.1.call-done = bf16[2048,2048]{1,0:T(8,128)(2,1)} async-done(((bf16[64,2048]{1,0:T(8,128)(2,1)}), bf16[2048,2048]{1,0:T(8,128)(2,1)}) %all-gather.2.cloned.1.call-update) | async-done | bytes 8388624 | tf_op jit(solution)/shard_map/all_gather | solution.py:23
  315.3 8.5 %fusion.2 = bf16[128,4,2048]{2,0,1:T(8,128)(2,1)S(1)} fusion(bf16[128,4,2048]{2,0,1:T(8,128)(2,1)} %dot_general.5, bf16[2048,2048]{1,0:T(8,128)(2,1)} %all-gather.2.cloned.1.call-done), kind=kOutput, calls=%fused_computation.4 | convolution fusion | flops 4296015872 | bytes 12582912 | tf_op jit(solution)/shard_map/dot_general | solution.py:21
  323.8 2.5 copy.16
  326.4 0.0 copy-start
  326.4 0.0 copy-start.1
  326.4 25.2 %all-to-all-start.1 = ((bf16[128,4,2048]{0,1,2:T(4,128)(2,1)}), bf16[128,4,2048]{0,1,2:T(4,128)(2,1)S(1)}, u32[]{:S(2)}, u32[]{:S(2)}) async-start(bf16[128,4,2048]{0,1,2:T(4,128)(2,1)} %copy.16), calls=%async_computation.1 | async-start | bytes 4194304 | tf_op jit(solution)/shard_map/all_to_all | solution.py:28
  351.6 0.8 dynamic_slice.7
  352.3 0.8 dynamic_slice.6
  353.1 0.0 copy-done
  353.1 0.0 copy-done.1
  353.1 0.2 multiply_reduce_fusion
  353.3 0.1 broadcast_add_fusion
  353.4 102.2 %all-to-all-done.1 = bf16[128,4,2048]{0,1,2:T(4,128)(2,1)S(1)} async-done(((bf16[128,4,2048]{0,1,2:T(4,128)(2,1)}), bf16[128,4,2048]{0,1,2:T(4,128)(2,1)S(1)}, u32[]{:S(2)}, u32[]{:S(2)}) %all-to-all-start.1) | async-done | bytes 2097184 | tf_op jit(solution)/shard_map/all_to_all | solution.py:28
  455.5 2.4 convert_bitcast_fusion
  457.9 6.4 %copy.17 = f32[128,16,4,128]{3,2,1,0:T(4,128)} copy(f32[128,16,4,128]{0,2,3,1:T(4,128)} %convert_bitcast_fusion) | data formatting | bytes 8388608 | tf_op jit(solution)/shard_map/convert_element_type | solution.py:40
  464.2 4.1 divide_convert_fusion
  (1 shorter events, 0.0 us)
Async XLA Ops:
  6.5 308.7 %all-gather.2.cloned.1.call-start = ((), (), s32[]{:S(2)}) async-start(), calls=%async_computation.2 | async-start | bytes 8650752 | tf_op jit(solution)/shard_map/all_gather | solution.py:23
  326.4 26.7 %copy-start = (s32[128,2]{0,1:T(2,128)S(1)}, s32[128,2]{0,1:T(2,128)}, u32[]{:S(2)}) copy-start(s32[128,2]{0,1:T(2,128)} %param.11) | copy-start | bytes 3076
  326.4 26.7 %copy-start.1 = (f32[128]{0:T(128)S(1)}, f32[128]{0:T(128)}, u32[]{:S(2)}) copy-start(f32[128]{0:T(128)} %param.12) | copy-start | bytes 1540
  326.4 129.2 %all-to-all-start.1 = ((bf16[128,4,2048]{0,1,2:T(4,128)(2,1)}), bf16[128,4,2048]{0,1,2:T(4,128)(2,1)S(1)}, u32[]{:S(2)}, u32[]{:S(2)}) async-start(bf16[128,4,2048]{0,1,2:T(4,128)(2,1)} %copy.16), calls=%async_computation.1 | async-start | bytes 4194304 | tf_op jit(solution)/shard_map/all_to_all | solution.py:28
Sparse Core Ops, SparseCore 0:
  9.4 305.8 all-gather.1
where the time goes:
time: 476 us; the launch traced here: 475 us
  waiting for transfers between devices  239 us (50%)
  blocking collectives  162 us (34%)
  starting transfers between devices  25.2 us (5%)
  local copies, waits for them, and re-layouts  14.4 us (3%)
  between operations  13.4 us (3%)
  other arithmetic  13.1 us (3%)
  matrix products  8.54 us (2%)
    all_to_all x1, blocking collectives, body(): lax.all_to_all(masked_amp, 'grp', split_axis=1, concat_axis=2, tiled=True)  162 us
    all_gather x1, waiting for transfers between devices, body(): lax.all_gather(masked_int, 'blk', axis=0, tiled=True)  136 us
    all_to_all x1, waiting for transfers between devices, body(): lax.all_to_all(ladder, 'grp', split_axis=2, concat_axis=1, tiled=True)  102 us
    all_to_all x1, starting transfers between devices, body(): lax.all_to_all(ladder, 'grp', split_axis=2, concat_axis=1, tiled=True)  25.2 us
  transfers between devices with their start and end apart: 2, of which 2 were waited for; matrix products, arithmetic and copies ran while one was open for 2% of the time, Pallas kernels for 0%

commit v1 on v0

v1 whole, which is shorter than its diff:
```python
import jax
import jax.numpy as jnp
from jax import lax
from jax.experimental import pallas as pl
from jax.experimental.pallas import tpu as pltpu
from jax.sharding import PartitionSpec as P

MESH = pl.DeviceIdType.MESH
TILE = 64
NX, NZ, NZL, NJ, NY, NC = 4, 16, 8, 8, 4, 2
CHUNKS = 16
AHEAD = 3
GROUP = 4


def drain(ref, sem):
    pltpu.make_async_copy(ref, ref, sem).wait()


def kernel(
    amp_ref,
    amp_map_ref,
    int_ref,
    int_map_ref,
    pair_ref,
    occ_ref,
    ve_smem,
    ve_row,
    out_ref,
    masked,
    ybuf,
    relay,
    zbuf,
    cbuf,
    bsend,
    bline,
    bfull,
    own_acc,
    erow,
    y_send,
    y_recv,
    z_send,
    z_recv,
    f_send,
    f_recv,
    c_send,
    c_recv,
    own_sem,
    bz_send,
    bz_recv,
    bx_send,
    bx_recv,
    by_send,
    by_recv,
    bc_send,
    bc_recv,
    in_sem,
):
    b = lax.axis_index("blk")
    g = lax.axis_index("grp")
    x, zl = b // NZL, b % NZL
    h, j = g // NJ, g % NJ
    y, c = j // NC, j % NC
    z = h * NZL + zl
    pairs = amp_ref.shape[0] // NJ
    q = pairs // CHUNKS
    half_cols = NJ * 128

    def at_z(zz):
        zz = (zz + NZ) % NZ
        return (x * NZL + zz % NZL, (zz // NZL) * NJ + j)

    def at_j(jj):
        return (b, h * NJ + jj)

    def at_x(xx):
        return (xx * NZL + zl, g)

    peers = [at_z(z + d) for d in (1, 2, 3, 4, -1, -2, -3, -4)]
    peers += [at_j((j + d) % NJ) for d in range(1, NJ)]
    peers += [at_x((x + d) % NX) for d in range(1, NX)]
    barrier = pltpu.get_barrier_semaphore()
    for peer in peers:
        pl.semaphore_signal(barrier, inc=1, device_id=peer, device_id_type=MESH)

    loads = [
        pltpu.make_async_copy(amp_ref, masked, in_sem.at[0]),
        pltpu.make_async_copy(
            int_ref.at[:, pl.ds(pl.multiple_of(j * 256, 128), 256)], bsend, in_sem.at[1]
        ),
    ]
    for load in loads:
        load.start()

    @pl.loop(0, TILE)
    def _(r):
        erow[pl.ds(r, 1), :] = jnp.full((1, 128), ve_smem[b * TILE + r], jnp.float32)

    lane = lax.broadcasted_iota(jnp.int32, (1, 128), 1)
    keep0 = amp_map_ref[0, 0].astype(jnp.float32)
    keep1 = amp_map_ref[0, 1].astype(jnp.float32)
    amp_mask = jnp.where(lane < TILE, keep0, keep1).astype(jnp.bfloat16)

    loads[0].wait()

    @pl.loop(0, NJ * pairs)
    def _(p):
        masked[p] = masked[p] * amp_mask

    ybuf[:, j] = masked[pl.ds(j * pairs, pairs)].reshape(CHUNKS, q, TILE, 128)
    loads[1].wait()
    for half in range(2):
        tile = 4 * j + 2 * half
        keep0 = int_map_ref[0, tile].astype(jnp.float32)
        keep1 = int_map_ref[0, tile + 1].astype(jnp.float32)
        int_mask = jnp.where(lane < TILE, keep0, keep1).astype(jnp.bfloat16)
        cols = slice(half * 128, half * 128 + 128)
        bsend[:, cols] = bsend[:, cols] * int_mask

    pl.semaphore_wait(barrier, len(peers))

    def send_chunk(k):
        for d in range(1, NJ):
            jj = (j + d) % NJ
            pltpu.make_async_remote_copy(
                src_ref=masked.at[pl.ds(jj * pairs + k * q, q)],
                dst_ref=ybuf.at[k, j],
                send_sem=y_send.at[k],
                recv_sem=y_recv.at[k],
                device_id=at_j(jj),
                device_id_type=MESH,
            ).start()

    send_chunk(0)

    in_half = x // 2 == h
    for i, d in enumerate((1, 2, 3, 4, -1, -2, -3)):
        zz = (z + d + NZ) % NZ

        @pl.when(zz // NZL == x // 2)
        def _():
            pltpu.make_async_remote_copy(
                src_ref=bsend,
                dst_ref=bline.at[zl],
                send_sem=bz_send.at[i],
                recv_sem=bz_recv,
                device_id=at_z(zz),
                device_id_type=MESH,
            ).start()

    for k in range(1, AHEAD):
        send_chunk(k)
    bline[zl] = bsend[...]

    def legs(k, first):
        src, dst = (ybuf, relay) if first else (relay, zbuf)
        ssem, rsem = (z_send, z_recv) if first else (f_send, f_recv)
        return [
            pltpu.make_async_remote_copy(
                src_ref=src.at[k, pl.ds(4 * way, 4)],
                dst_ref=dst.at[k, pl.ds(4 * way, 4)],
                send_sem=ssem.at[k, way],
                recv_sem=rsem.at[k, way],
                device_id=at_z(z + (4 if way == 0 else -4)),
                device_id_type=MESH,
            )
            for way in range(2)
        ]

    def b_along_x():
        @pl.when(in_half)
        def _():
            drain(bline.at[pl.ds(0, NZL - 1)], bz_recv)
            bfull[y, c, x % 2] = bline[...].reshape(NZL * TILE, 256).T
            for d in range(1, NX):
                pltpu.make_async_remote_copy(
                    src_ref=bfull.at[y, c, x % 2],
                    dst_ref=bfull.at[y, c, x % 2],
                    send_sem=bx_send.at[d - 1],
                    recv_sem=bx_recv.at[x % 2],
                    device_id=at_x((x + d) % NX),
                    device_id_type=MESH,
                ).start()

    def b_along_y():
        for xx in range(2):

            @pl.when(x != 2 * h + xx)
            def _():
                drain(bfull.at[y, c, xx], bx_recv.at[xx])

        for d in range(1, NY):
            pltpu.make_async_remote_copy(
                src_ref=bfull.at[y, c],
                dst_ref=bfull.at[y, c],
                send_sem=by_send.at[d - 1],
                recv_sem=by_recv.at[y],
                device_id=at_j(((y + d) % NY) * NC + c),
                device_id_type=MESH,
            ).start()

    def b_core():
        for d in range(1, NY):
            yy = (y + d) % NY
            drain(bfull.at[yy, c], by_recv.at[yy])
        return b_core_copies()

    def b_core_copies():
        return [
            pltpu.make_async_remote_copy(
                src_ref=bfull.at[yy, c],
                dst_ref=bfull.at[yy, c],
                send_sem=bc_send.at[yy],
                recv_sem=bc_recv.at[yy],
                device_id=at_j(y * NC + 1 - c),
                device_id_type=MESH,
            )
            for yy in range(NY)
        ]

    def weights(hh, i, n):
        cols = pl.ds(pl.multiple_of((n % 2) * 256, 256), 256)
        return bfull[2 * hh + i // 2, i % 2, n // 2, :, cols]

    def rows_of(buf, first, count, i):
        blocks = [
            buf[pl.ds(first, count), 2 * i + e].reshape(count * q * TILE, 128) for e in range(2)
        ]
        return jnp.concatenate(blocks, axis=1)

    def own_half(group):
        @pl.loop(0, 4)
        def _(n):
            acc = jnp.zeros((GROUP * q * TILE, 256), jnp.float32)
            for i in range(4):
                acc += jnp.dot(
                    rows_of(ybuf, group * GROUP, GROUP, i),
                    weights(h, i, n),
                    preferred_element_type=jnp.float32,
                )
            own_acc[n, pl.ds(group * GROUP, GROUP)] = acc.reshape(GROUP, q * TILE, 256)

    def compute(k):
        @pl.loop(0, 4)
        def _(n):
            acc = own_acc[n, k]
            for i in range(4):
                acc += jnp.dot(
                    rows_of(zbuf, k, 1, i),
                    weights(1 - h, i, n),
                    preferred_element_type=jnp.float32,
                )
            ladder = acc.astype(jnp.bfloat16).astype(jnp.float32)
            for e in range(2):
                start = pl.multiple_of(h * half_cols + n * 256 + e * 128, 128)
                virt = erow[...] + ve_row[:, pl.ds(start, 128)]
                for p in range(q):
                    pair = j * pairs + k * q + p
                    shift = occ_ref[pair_ref[0, pair]] + occ_ref[pair_ref[1, pair]]
                    block = ladder[p * TILE : (p + 1) * TILE, e * 128 : (e + 1) * 128]
                    cbuf[k, 2 * n + e, p] = (block / (virt - shift)).astype(jnp.bfloat16)

        for d in range(1, NJ):
            jj = (j + d) % NJ
            pltpu.make_async_remote_copy(
                src_ref=cbuf.at[k, jj],
                dst_ref=out_ref.at[pl.ds(j * pairs + k * q, q)],
                send_sem=c_send.at[k],
                recv_sem=c_recv,
                device_id=at_j(jj),
                device_id_type=MESH,
            ).start()
        own_copy(k).start()

    def own_copy(k):
        return pltpu.make_async_copy(
            cbuf.at[k, j], out_ref.at[pl.ds(j * pairs + k * q, q)], own_sem.at[k]
        )

    lag1, lag2 = 2, 4

    @pl.loop(0, CHUNKS + lag2)
    def _(t):
        @pl.when(t + AHEAD < CHUNKS)
        def _():
            send_chunk(t + AHEAD)

        @pl.when(t < CHUNKS)
        def _():
            drain(ybuf.at[t, pl.ds(0, NJ - 1)], y_recv.at[t])
            for copy in legs(t, True):
                copy.start()

        @pl.when(t == 1)
        def _():
            b_along_x()

        @pl.when(jnp.logical_and(t >= lag1, t < CHUNKS + lag1))
        def _():
            k = t - lag1
            first, second = legs(k, True), legs(k, False)
            for way in range(2):
                first[way].wait_recv()
                second[way].start()

        @pl.when(t == 2)
        def _():
            b_along_y()

        @pl.when(t == 3)
        def _():
            for copy in b_core():
                copy.start()

        @pl.when(t == lag2)
        def _():
            other = 1 - c
            for yy in range(NY):
                drain(bfull.at[yy, other], bc_recv.at[yy])

        @pl.when(t >= lag2)
        def _():
            k = t - lag2

            @pl.when(k % GROUP == 0)
            def _():
                own_half(k // GROUP)

            for copy in legs(k, False):
                copy.wait_recv()
            compute(k)

    drain(out_ref.at[pl.ds(0, (NJ - 1) * pairs)], c_recv)

    @pl.loop(0, CHUNKS)
    def _(k):
        drain(ybuf.at[k, pl.ds(0, NJ - 1)], y_send.at[k])
        for copy in legs(k, True) + legs(k, False):
            copy.wait_send()
        drain(cbuf.at[k, pl.ds(0, NJ - 1)], c_send.at[k])
        own_copy(k).wait()

    for i, d in enumerate((1, 2, 3, 4, -1, -2, -3)):
        zz = (z + d + NZ) % NZ

        @pl.when(zz // NZL == x // 2)
        def _():
            drain(bsend, bz_send.at[i])

    @pl.when(in_half)
    def _():
        for d in range(1, NX):
            drain(bfull.at[y, c, x % 2], bx_send.at[d - 1])

    for d in range(1, NY):
        drain(bfull.at[y, c], by_send.at[d - 1])
    for copy in b_core_copies():
        copy.wait_send()


def body(
    amplitudes, amplitude_map, integrals, integral_map, pair_list, occupied_energy, virtual_energy
):
    pair_count, rows, cols = amplitudes.shape
    q = pair_count // NJ // CHUNKS
    vmem = pl.BlockSpec(memory_space=pltpu.VMEM)
    hbm = pl.BlockSpec(memory_space=pl.ANY)
    smem = pl.BlockSpec(memory_space=pltpu.SMEM)
    dma = pltpu.SemaphoreType.DMA
    block = pltpu.VMEM((CHUNKS, NJ, q, rows, cols), jnp.bfloat16)
    return pl.pallas_call(
        kernel,
        out_shape=jax.ShapeDtypeStruct(amplitudes.shape, jnp.bfloat16),
        in_specs=[hbm, smem, hbm, smem, smem, smem, smem, vmem],
        out_specs=pl.BlockSpec(memory_space=pl.ANY),
        scratch_shapes=[
            pltpu.VMEM(amplitudes.shape, jnp.bfloat16),
            block,
            block,
            block,
            block,
            pltpu.VMEM((TILE, 256), jnp.bfloat16),
            pltpu.VMEM((NZL, TILE, 256), jnp.bfloat16),
            pltpu.VMEM((NY, NC, 2, 256, NZL * TILE), jnp.bfloat16),
            pltpu.VMEM((4, CHUNKS, q * rows, 256), jnp.float32),
            pltpu.VMEM((TILE, 128), jnp.float32),
            dma((CHUNKS,)),
            dma((CHUNKS,)),
            dma((CHUNKS, 2)),
            dma((CHUNKS, 2)),
            dma((CHUNKS, 2)),
            dma((CHUNKS, 2)),
            dma((CHUNKS,)),
            dma,
            dma((CHUNKS,)),
            dma((7,)),
            dma,
            dma((NX - 1,)),
            dma((2,)),
            dma((NY - 1,)),
            dma((NY,)),
            dma((NY,)),
            dma((NY,)),
            dma((2,)),
        ],
        compiler_params=pltpu.CompilerParams(
            collective_id=0, has_side_effects=True, vmem_limit_bytes=60 * 1024 * 1024
        ),
        cost_estimate=pl.CostEstimate(
            flops=2 * 1024 * 2048 * 1024, bytes_accessed=8 * 1024 * 1024, transcendentals=0
        ),
    )(
        amplitudes,
        amplitude_map,
        integrals,
        integral_map,
        pair_list.T,
        occupied_energy,
        virtual_energy,
        virtual_energy.reshape(1, -1),
    )


def solution(mesh):
    in_specs = (
        P(None, "blk", "grp"),
        P("blk", "grp"),
        P("blk", None),
        P("blk", None),
        P(),
        P(),
        P(),
    )
    out_specs = P(None, "blk", "grp")
    return jax.shard_map(body, mesh=mesh, in_specs=in_specs, out_specs=out_specs, check_vma=False)
```

time: 476 us -> 230 us (0.48)
  the two profiles are of different devices: /device:TPU:121 before, /device:TPU:1 now
where the time goes in v1:
time: 230 us; the launch traced here: 227 us
  Pallas kernels  224 us (97%)
  local copies, waits for them, and re-layouts  3.08 us (1%)
    pallas_call x1, Pallas kernels, body(): pl.pallas_call(kernel, out_shape=jax.ShapeDtypeStruct(amplitudes.shape, j...  224 us

profile of v1, /device:TPU:1, one launch (start us, length us, event | category | flops | bytes accessed | tf_op | source)
XLA Modules:
  0.0 227.0 jit_solution(14559005378797757787)
XLA Ops:
  0.0 223.9 %shard_map.73 = bf16[128,64,128]{2,1,0:T(8,128)(2,1)} custom-call(bf16[128,64,128]{2,1,0:T(8,128)(2,1)} %amp_ref.1, s32[1,2]{1,0:T(1,128)} %amp_map_ref.1, bf16[64,2048]{1,0:T(8,128)(2,1)} %int_ref.1, s32[1,32]{1,0:T(1,128)} %int_map_ref.1, s32[2,128]{1,0:T(2,128)} %bitcast.3, f32[128]{0:T(128)} %occ_ref.1, f32[2048]{0:T(1024)} %ve_smem.1, f32[1,2048]{1,0:T(1,128)} %bitcast.2), custom_call_target="tpu_custom_call" | custom-call | flops 4294967296 | bytes 8388608 | tf_op jit(solution)/shard_map/pallas_call | solution.py:371
  223.9 3.1 %copy.9 = bf16[128,64,128]{2,1,0:T(8,128)(2,1)} copy(bf16[128,64,128]{2,1,0:T(8,128)(2,1)} %shard_map.73) | data formatting | bytes 4194304

commit v2 on v1

--- a/solution.py
+++ b/solution.py
@@ -11,6 +11,7 @@
 CHUNKS = 16
 AHEAD = 3
 GROUP = 4
+HOPS, LAG = 8, 2
 
 
 def drain(ref, sem):
@@ -28,9 +29,7 @@
     ve_row,
     out_ref,
     masked,
-    ybuf,
-    relay,
-    zbuf,
+    zall,
     cbuf,
     bsend,
     bline,
@@ -41,8 +40,6 @@
     y_recv,
     z_send,
     z_recv,
-    f_send,
-    f_recv,
     c_send,
     c_recv,
     own_sem,
@@ -76,6 +73,8 @@
     def at_x(xx):
         return (xx * NZL + zl, g)
 
+    ybuf, zbuf = zall.at[0], zall.at[HOPS]
+
     peers = [at_z(z + d) for d in (1, 2, 3, 4, -1, -2, -3, -4)]
     peers += [at_j((j + d) % NJ) for d in range(1, NJ)]
     peers += [at_x((x + d) % NX) for d in range(1, NX)]
@@ -152,20 +151,15 @@
         send_chunk(k)
     bline[zl] = bsend[...]
 
-    def legs(k, first):
-        src, dst = (ybuf, relay) if first else (relay, zbuf)
-        ssem, rsem = (z_send, z_recv) if first else (f_send, f_recv)
-        return [
-            pltpu.make_async_remote_copy(
-                src_ref=src.at[k, pl.ds(4 * way, 4)],
-                dst_ref=dst.at[k, pl.ds(4 * way, 4)],
-                send_sem=ssem.at[k, way],
-                recv_sem=rsem.at[k, way],
-                device_id=at_z(z + (4 if way == 0 else -4)),
-                device_id_type=MESH,
-            )
-            for way in range(2)
-        ]
+    def hop(m, k, way):
+        return pltpu.make_async_remote_copy(
+            src_ref=zall.at[m - 1, k, pl.ds(4 * way, 4)],
+            dst_ref=zall.at[m, k, pl.ds(4 * way, 4)],
+            send_sem=z_send.at[m - 1, k, way],
+            recv_sem=z_recv.at[m - 1, k, way],
+            device_id=at_z(z + (1 if way == 0 else -1)),
+            device_id_type=MESH,
+        )
 
     def b_along_x():
         @pl.when(in_half)
@@ -277,57 +271,51 @@
             cbuf.at[k, j], out_ref.at[pl.ds(j * pairs + k * q, q)], own_sem.at[k]
         )
 
-    lag1, lag2 = 2, 4
-
-    @pl.loop(0, CHUNKS + lag2)
-    def _(t):
-        @pl.when(t + AHEAD < CHUNKS)
-        def _():
-            send_chunk(t + AHEAD)
-
-        @pl.when(t < CHUNKS)
-        def _():
-            drain(ybuf.at[t, pl.ds(0, NJ - 1)], y_recv.at[t])
-            for copy in legs(t, True):
-                copy.start()
-
-        @pl.when(t == 1)
+    @pl.loop(0, CHUNKS + LAG * HOPS)
+    def _(s):
+        @pl.when(s + AHEAD < CHUNKS)
+        def _():
+            send_chunk(s + AHEAD)
+
+        for m in range(HOPS, 0, -1):
+            k = s - LAG * (m - 1)
+
+            @pl.when(jnp.logical_and(k >= 0, k < CHUNKS))
+            def _():
+                if m == 1:
+                    drain(ybuf.at[k, pl.ds(0, NJ - 1)], y_recv.at[k])
+                for way in range(2):
+                    if m > 1:
+                        hop(m - 1, k, way).wait_recv()
+                    hop(m, k, way).start()
+
+        @pl.when(s == 4)
         def _():
             b_along_x()
 
-        @pl.when(jnp.logical_and(t >= lag1, t < CHUNKS + lag1))
-        def _():
-            k = t - lag1
-            first, second = legs(k, True), legs(k, False)
-            for way in range(2):
-                first[way].wait_recv()
-                second[way].start()
-
-        @pl.when(t == 2)
+        @pl.when(s == 6)
         def _():
             b_along_y()
 
-        @pl.when(t == 3)
+        @pl.when(s == 9)
         def _():
             for copy in b_core():
                 copy.start()
 
-        @pl.when(t == lag2)
-        def _():
-            other = 1 - c
+        @pl.when(s == 11)
+        def _():
             for yy in range(NY):
-                drain(bfull.at[yy, other], bc_recv.at[yy])
-
-        @pl.when(t >= lag2)
-        def _():
-            k = t - lag2
-
-            @pl.when(k % GROUP == 0)
-            def _():
-                own_half(k // GROUP)
-
-            for copy in legs(k, False):
-                copy.wait_recv()
+                drain(bfull.at[yy, 1 - c], bc_recv.at[yy])
+
+        @pl.when(jnp.logical_and(s >= 12, s < 12 + CHUNKS // GROUP))
+        def _():
+            own_half(s - 12)
+
+        @pl.when(s >= LAG * HOPS)
+        def _():
+            k = s - LAG * HOPS
+            for way in range(2):
+                hop(HOPS, k, way).wait_recv()
             compute(k)
 
     drain(out_ref.at[pl.ds(0, (NJ - 1) * pairs)], c_recv)
@@ -335,8 +323,9 @@
     @pl.loop(0, CHUNKS)
     def _(k):
         drain(ybuf.at[k, pl.ds(0, NJ - 1)], y_send.at[k])
-        for copy in legs(k, True) + legs(k, False):
-            copy.wait_send()
+        for m in range(1, HOPS + 1):
+            for way in range(2):
+                hop(m, k, way).wait_send()
         drain(cbuf.at[k, pl.ds(0, NJ - 1)], c_send.at[k])
         own_copy(k).wait()
 
@@ -367,7 +356,7 @@
     hbm = pl.BlockSpec(memory_space=pl.ANY)
     smem = pl.BlockSpec(memory_space=pltpu.SMEM)
     dma = pltpu.SemaphoreType.DMA
-    block = pltpu.VMEM((CHUNKS, NJ, q, rows, cols), jnp.bfloat16)
+    block = (CHUNKS, NJ, q, rows, cols)
     return pl.pallas_call(
         kernel,
         out_shape=jax.ShapeDtypeStruct(amplitudes.shape, jnp.bfloat16),
@@ -375,10 +364,8 @@
         out_specs=pl.BlockSpec(memory_space=pl.ANY),
         scratch_shapes=[
             pltpu.VMEM(amplitudes.shape, jnp.bfloat16),
-            block,
-            block,
-            block,
-            block,
+            pltpu.VMEM((HOPS + 1, *block), jnp.bfloat16),
+            pltpu.VMEM(block, jnp.bfloat16),
             pltpu.VMEM((TILE, 256), jnp.bfloat16),
             pltpu.VMEM((NZL, TILE, 256), jnp.bfloat16),
             pltpu.VMEM((NY, NC, 2, 256, NZL * TILE), jnp.bfloat16),
@@ -386,10 +373,8 @@
             pltpu.VMEM((TILE, 128), jnp.float32),
             dma((CHUNKS,)),
             dma((CHUNKS,)),
-            dma((CHUNKS, 2)),
-            dma((CHUNKS, 2)),
-            dma((CHUNKS, 2)),
-            dma((CHUNKS, 2)),
+            dma((HOPS, CHUNKS, 2)),
+            dma((HOPS, CHUNKS, 2)),
             dma((CHUNKS,)),
             dma,
             dma((CHUNKS,)),

time: 230 us -> 224 us (0.974); the launches traced: 227 us -> 224 us
  Pallas kernels: 224 us -> 221 us
    pallas_call x1, Pallas kernels: 224 us -> 221 us  [body(): pl.pallas_call(kernel, out_shape=jax.ShapeDtypeStruct(amplitudes.shape, j...]
where the time goes in v2:
time: 224 us
  Pallas kernels  221 us (99%)
  local copies, waits for them, and re-layouts  3.08 us (1%)
    pallas_call x1, Pallas kernels, body(): pl.pallas_call(kernel, out_shape=jax.ShapeDtypeStruct(amplitudes.shape, j...  221 us

profile of v2, /device:TPU:1, one launch (start us, length us, event | category | flops | bytes accessed | tf_op | source)
XLA Modules:
  0.0 223.7 jit_solution(8054993045905248883)
XLA Ops:
  0.0 220.6 %shard_map.73 = bf16[128,64,128]{2,1,0:T(8,128)(2,1)} custom-call(bf16[128,64,128]{2,1,0:T(8,128)(2,1)} %amp_ref.1, s32[1,2]{1,0:T(1,128)} %amp_map_ref.1, bf16[64,2048]{1,0:T(8,128)(2,1)} %int_ref.1, s32[1,32]{1,0:T(1,128)} %int_map_ref.1, s32[2,128]{1,0:T(2,128)} %bitcast.3, f32[128]{0:T(128)} %occ_ref.1, f32[2048]{0:T(1024)} %ve_smem.1, f32[1,2048]{1,0:T(1,128)} %bitcast.2), custom_call_target="tpu_custom_call" | custom-call | flops 4294967296 | bytes 8388608 | tf_op jit(solution)/shard_map/pallas_call | solution.py:360
  220.7 3.1 %copy.9 = bf16[128,64,128]{2,1,0:T(8,128)(2,1)} copy(bf16[128,64,128]{2,1,0:T(8,128)(2,1)} %shard_map.73) | data formatting | bytes 4194304

commit v3 on v1

--- a/solution.py
+++ b/solution.py
@@ -8,9 +8,10 @@
 MESH = pl.DeviceIdType.MESH
 TILE = 64
 NX, NZ, NZL, NJ, NY, NC = 4, 16, 8, 8, 4, 2
-CHUNKS = 16
+CHUNKS = 8
 AHEAD = 3
-GROUP = 4
+GROUP = 2
+LEGS = (5, 3)
 
 
 def drain(ref, sem):
@@ -32,7 +33,6 @@
     relay,
     zbuf,
     cbuf,
-    bsend,
     bline,
     bfull,
     own_acc,
@@ -76,7 +76,7 @@
     def at_x(xx):
         return (xx * NZL + zl, g)
 
-    peers = [at_z(z + d) for d in (1, 2, 3, 4, -1, -2, -3, -4)]
+    peers = [at_z(z + d) for d in (1, -1, 3, -3, 5, -5)]
     peers += [at_j((j + d) % NJ) for d in range(1, NJ)]
     peers += [at_x((x + d) % NX) for d in range(1, NX)]
     barrier = pltpu.get_barrier_semaphore()
@@ -86,7 +86,7 @@
     loads = [
         pltpu.make_async_copy(amp_ref, masked, in_sem.at[0]),
         pltpu.make_async_copy(
-            int_ref.at[:, pl.ds(pl.multiple_of(j * 256, 128), 256)], bsend, in_sem.at[1]
+            int_ref.at[:, pl.ds(pl.multiple_of(j * 256, 128), 256)], bline.at[zl], in_sem.at[1]
         ),
     ]
     for load in loads:
@@ -115,7 +115,7 @@
         keep1 = int_map_ref[0, tile + 1].astype(jnp.float32)
         int_mask = jnp.where(lane < TILE, keep0, keep1).astype(jnp.bfloat16)
         cols = slice(half * 128, half * 128 + 128)
-        bsend[:, cols] = bsend[:, cols] * int_mask
+        bline[zl, :, cols] = bline[zl, :, cols] * int_mask
 
     pl.semaphore_wait(barrier, len(peers))
 
@@ -133,27 +133,33 @@
 
     send_chunk(0)
 
-    in_half = x // 2 == h
-    for i, d in enumerate((1, 2, 3, 4, -1, -2, -3)):
-        zz = (z + d + NZ) % NZ
-
-        @pl.when(zz // NZL == x // 2)
-        def _():
-            pltpu.make_async_remote_copy(
-                src_ref=bsend,
-                dst_ref=bline.at[zl],
-                send_sem=bz_send.at[i],
-                recv_sem=bz_recv,
-                device_id=at_z(zz),
-                device_id_type=MESH,
-            ).start()
-
+    def b_hop(r, way):
+        step = 1 if way == 0 else -1
+        slot = (z - step * (r - 1) + NZ) % NZL
+        return pltpu.make_async_remote_copy(
+            src_ref=bline.at[slot],
+            dst_ref=bline.at[slot],
+            send_sem=bz_send.at[4 * way + r - 1],
+            recv_sem=bz_recv.at[4 * way + r - 1],
+            device_id=at_z(z + step),
+            device_id_type=MESH,
+        )
+
+    def b_arrived(r, way):
+        step = 1 if way == 0 else -1
+        drain(bline.at[(z - step * r + NZ) % NZL], bz_recv.at[4 * way + r - 1])
+
+    for way in range(2):
+        b_hop(1, way).start()
     for k in range(1, AHEAD):
         send_chunk(k)
-    bline[zl] = bsend[...]
+        for way in range(2):
+            b_arrived(k, way)
+            b_hop(k + 1, way).start()
 
     def legs(k, first):
         src, dst = (ybuf, relay) if first else (relay, zbuf)
+        hops = LEGS[0] if first else LEGS[1]
         ssem, rsem = (z_send, z_recv) if first else (f_send, f_recv)
         return [
             pltpu.make_async_remote_copy(
@@ -161,16 +167,19 @@
                 dst_ref=dst.at[k, pl.ds(4 * way, 4)],
                 send_sem=ssem.at[k, way],
                 recv_sem=rsem.at[k, way],
-                device_id=at_z(z + (4 if way == 0 else -4)),
+                device_id=at_z(z + (hops if way == 0 else -hops)),
                 device_id_type=MESH,
             )
             for way in range(2)
         ]
 
+    in_half = x // 2 == h
+
     def b_along_x():
+        b_arrived(4, 0)
+
         @pl.when(in_half)
         def _():
-            drain(bline.at[pl.ds(0, NZL - 1)], bz_recv)
             bfull[y, c, x % 2] = bline[...].reshape(NZL * TILE, 256).T
             for d in range(1, NX):
                 pltpu.make_async_remote_copy(
@@ -291,6 +300,12 @@
             for copy in legs(t, True):
                 copy.start()
 
+        @pl.when(t == 0)
+        def _():
+            b_arrived(3, 0)
+            b_arrived(3, 1)
+            b_hop(4, 0).start()
+
         @pl.when(t == 1)
         def _():
             b_along_x()
@@ -340,12 +355,9 @@
         drain(cbuf.at[k, pl.ds(0, NJ - 1)], c_send.at[k])
         own_copy(k).wait()
 
-    for i, d in enumerate((1, 2, 3, 4, -1, -2, -3)):
-        zz = (z + d + NZ) % NZ
-
-        @pl.when(zz // NZL == x // 2)
-        def _():
-            drain(bsend, bz_send.at[i])
+    for way in range(2):
+        for r in range(1, 5 - way):
+            b_hop(r, way).wait_send()
 
     @pl.when(in_half)
     def _():
@@ -379,7 +391,6 @@
             block,
             block,
             block,
-            pltpu.VMEM((TILE, 256), jnp.bfloat16),
             pltpu.VMEM((NZL, TILE, 256), jnp.bfloat16),
             pltpu.VMEM((NY, NC, 2, 256, NZL * TILE), jnp.bfloat16),
             pltpu.VMEM((4, CHUNKS, q * rows, 256), jnp.float32),
@@ -394,7 +405,7 @@
             dma,
             dma((CHUNKS,)),
             dma((7,)),
-            dma,
+            dma((7,)),
             dma((NX - 1,)),
             dma((2,)),
             dma((NY - 1,)),

time: 230 us -> 215 us (0.935)
  Pallas kernels: 224 us -> 211 us
    pallas_call x1, Pallas kernels: 224 us -> 211 us  [body(): pl.pallas_call(kernel, out_shape=jax.ShapeDtypeStruct(amplitudes.shape, j...]
where the time goes in v3:
time: 215 us; the launch traced here: 214 us
  Pallas kernels  211 us (98%)
  local copies, waits for them, and re-layouts  3.08 us (1%)
    pallas_call x1, Pallas kernels, body(): pl.pallas_call(kernel, out_shape=jax.ShapeDtypeStruct(amplitudes.shape, j...  211 us

profile of v3, /device:TPU:1, one launch (start us, length us, event | category | flops | bytes accessed | tf_op | source)
XLA Modules:
  0.0 214.2 jit_solution(14820361867362510095)
XLA Ops:
  0.0 211.1 %shard_map.73 = bf16[128,64,128]{2,1,0:T(8,128)(2,1)} custom-call(bf16[128,64,128]{2,1,0:T(8,128)(2,1)} %amp_ref.1, s32[1,2]{1,0:T(1,128)} %amp_map_ref.1, bf16[64,2048]{1,0:T(8,128)(2,1)} %int_ref.1, s32[1,32]{1,0:T(1,128)} %int_map_ref.1, s32[2,128]{1,0:T(2,128)} %bitcast.3, f32[128]{0:T(128)} %occ_ref.1, f32[2048]{0:T(1024)} %ve_smem.1, f32[1,2048]{1,0:T(1,128)} %bitcast.2), custom_call_target="tpu_custom_call" | custom-call | flops 4294967296 | bytes 8388608 | tf_op jit(solution)/shard_map/pallas_call | solution.py:383
  211.1 3.1 %copy.9 = bf16[128,64,128]{2,1,0:T(8,128)(2,1)} copy(bf16[128,64,128]{2,1,0:T(8,128)(2,1)} %shard_map.73) | data formatting | bytes 4194304

commit v4 on v3

--- a/solution.py
+++ b/solution.py
@@ -8,9 +8,9 @@
 MESH = pl.DeviceIdType.MESH
 TILE = 64
 NX, NZ, NZL, NJ, NY, NC = 4, 16, 8, 8, 4, 2
-CHUNKS = 8
-AHEAD = 3
-GROUP = 2
+CHUNKS = 16
+AHEAD = 4
+GROUP = 4
 LEGS = (5, 3)
 
 
@@ -153,9 +153,6 @@
         b_hop(1, way).start()
     for k in range(1, AHEAD):
         send_chunk(k)
-        for way in range(2):
-            b_arrived(k, way)
-            b_hop(k + 1, way).start()
 
     def legs(k, first):
         src, dst = (ybuf, relay) if first else (relay, zbuf)
@@ -251,7 +248,8 @@
 
     def compute(k):
         @pl.loop(0, 4)
-        def _(n):
+        def _(step):
+            n = (step + y) % 4
             acc = own_acc[n, k]
             for i in range(4):
                 acc += jnp.dot(
@@ -269,16 +267,20 @@
                     block = ladder[p * TILE : (p + 1) * TILE, e * 128 : (e + 1) * 128]
                     cbuf[k, 2 * n + e, p] = (block / (virt - shift)).astype(jnp.bfloat16)
 
-        for d in range(1, NJ):
-            jj = (j + d) % NJ
-            pltpu.make_async_remote_copy(
-                src_ref=cbuf.at[k, jj],
-                dst_ref=out_ref.at[pl.ds(j * pairs + k * q, q)],
-                send_sem=c_send.at[k],
-                recv_sem=c_recv,
-                device_id=at_j(jj),
-                device_id_type=MESH,
-            ).start()
+            for e in range(2):
+                jj = 2 * n + e
+
+                @pl.when(jj != j)
+                def _():
+                    pltpu.make_async_remote_copy(
+                        src_ref=cbuf.at[k, jj],
+                        dst_ref=out_ref.at[pl.ds(j * pairs + k * q, q)],
+                        send_sem=c_send.at[k],
+                        recv_sem=c_recv,
+                        device_id=at_j(jj),
+                        device_id_type=MESH,
+                    ).start()
+
         own_copy(k).start()
 
     def own_copy(k):
@@ -286,7 +288,7 @@
             cbuf.at[k, j], out_ref.at[pl.ds(j * pairs + k * q, q)], own_sem.at[k]
         )
 
-    lag1, lag2 = 2, 4
+    lag1, lag2 = 8, 16
 
     @pl.loop(0, CHUNKS + lag2)
     def _(t):
@@ -300,13 +302,16 @@
             for copy in legs(t, True):
                 copy.start()
 
-        @pl.when(t == 0)
-        def _():
-            b_arrived(3, 0)
-            b_arrived(3, 1)
-            b_hop(4, 0).start()
-
-        @pl.when(t == 1)
+        for r in range(1, 4):
+
+            @pl.when(t == r - 1)
+            def _():
+                for way in range(2):
+                    b_arrived(r, way)
+                    if r + way < 4:
+                        b_hop(r + 1, way).start()
+
+        @pl.when(t == 3)
         def _():
             b_along_x()
 
@@ -318,29 +323,28 @@
                 first[way].wait_recv()
                 second[way].start()
 
-        @pl.when(t == 2)
+        @pl.when(t == 6)
         def _():
             b_along_y()
 
-        @pl.when(t == 3)
+        @pl.when(t == 9)
         def _():
             for copy in b_core():
                 copy.start()
 
-        @pl.when(t == lag2)
+        @pl.when(t == 12)
         def _():
             other = 1 - c
             for yy in range(NY):
                 drain(bfull.at[yy, other], bc_recv.at[yy])
 
+        @pl.when(jnp.logical_and(t >= 12, t < 12 + CHUNKS // GROUP))
+        def _():
+            own_half(t - 12)
+
         @pl.when(t >= lag2)
         def _():
             k = t - lag2
-
-            @pl.when(k % GROUP == 0)
-            def _():
-                own_half(k // GROUP)
-
             for copy in legs(k, False):
                 copy.wait_recv()
             compute(k)
@@ -368,6 +372,10 @@
         drain(bfull.at[y, c], by_send.at[d - 1])
     for copy in b_core_copies():
         copy.wait_send()
+
+
+def copy_out(src_ref, dst_ref):
+    dst_ref[...] = src_ref[...]
 
 
 def body(
@@ -380,7 +388,7 @@
     smem = pl.BlockSpec(memory_space=pltpu.SMEM)
     dma = pltpu.SemaphoreType.DMA
     block = pltpu.VMEM((CHUNKS, NJ, q, rows, cols), jnp.bfloat16)
-    return pl.pallas_call(
+    update = pl.pallas_call(
         kernel,
         out_shape=jax.ShapeDtypeStruct(amplitudes.shape, jnp.bfloat16),
         in_specs=[hbm, smem, hbm, smem, smem, smem, smem, vmem],
@@ -430,6 +438,15 @@
         virtual_energy,
         virtual_energy.reshape(1, -1),
     )
+    part = pl.BlockSpec((pair_count // 8, rows, cols), lambda i: (i, 0, 0))
+    return pl.pallas_call(
+        copy_out,
+        grid=(8,),
+        out_shape=jax.ShapeDtypeStruct(amplitudes.shape, jnp.bfloat16),
+        in_specs=[part],
+        out_specs=part,
+        compiler_params=pltpu.CompilerParams(vmem_limit_bytes=60 * 1024 * 1024),
+    )(update)
 
 
 def solution(mesh):

time: 215 us -> 218 us (1.014)
  Pallas kernels: 211 us -> 218 us
  local copies, waits for them, and re-layouts: 3.08 us -> 0 us
    pallas_call x0 -> x1, Pallas kernels: none -> 5.64 us  [body(): pl.pallas_call(copy_out, grid=(8,), out_shape=jax.ShapeDtypeStruct(amplit...]
    unnamed x1 -> x0, local copies, waits for them, and re-layouts: 3.08 us -> none
where the time goes in v4:
time: 218 us
  Pallas kernels  218 us (100%)
    pallas_call x1, Pallas kernels, body(): pl.pallas_call(kernel, out_shape=jax.ShapeDtypeStruct(amplitudes.shape, j...  212 us
    pallas_call x1, Pallas kernels, body(): pl.pallas_call(copy_out, grid=(8,), out_shape=jax.ShapeDtypeStruct(amplit...  5.64 us

profile of v4, /device:TPU:1, one launch (start us, length us, event | category | flops | bytes accessed | tf_op | source)
XLA Modules:
  0.0 217.8 jit_solution(17021946907636600324)
XLA Ops:
  0.0 212.2 %shard_map.73.src_ref = bf16[128,64,128]{2,1,0:T(8,128)(2,1)} custom-call(bf16[128,64,128]{2,1,0:T(8,128)(2,1)} %amp_ref.1, s32[1,2]{1,0:T(1,128)} %amp_map_ref.1, bf16[64,2048]{1,0:T(8,128)(2,1)} %int_ref.1, s32[1,32]{1,0:T(1,128)} %int_map_ref.1, s32[2,128]{1,0:T(2,128)} %bitcast.3, f32[128]{0:T(128)} %occ_ref.1, f32[2048]{0:T(1024)} %ve_smem.1, ...), custom_call_target="tpu_custom_call" | custom-call | flops 4294967296 | bytes 8388608 | tf_op jit(solution)/shard_map/pallas_call | solution.py:391
  212.2 5.6 %shard_map.74 = bf16[128,64,128]{2,1,0:T(8,128)(2,1)} custom-call(bf16[128,64,128]{2,1,0:T(8,128)(2,1)} %shard_map.73.src_ref), custom_call_target="tpu_custom_call" | custom-call | tf_op jit(solution)/shard_map/pallas_call | solution.py:442

commit v5 on v4

--- a/solution.py
+++ b/solution.py
@@ -9,7 +9,7 @@
 TILE = 64
 NX, NZ, NZL, NJ, NY, NC = 4, 16, 8, 8, 4, 2
 CHUNKS = 16
-AHEAD = 4
+AHEAD = 2
 GROUP = 4
 LEGS = (5, 3)
 
@@ -19,15 +19,21 @@
 
 
 def kernel(
-    amp_ref,
+    amp_hbm,
+    amp_map_hbm,
+    int_hbm,
+    int_map_hbm,
+    pair_hbm,
+    occ_hbm,
+    ve_hbm,
+    ve_row_hbm,
+    out_ref,
     amp_map_ref,
-    int_ref,
     int_map_ref,
     pair_ref,
     occ_ref,
     ve_smem,
     ve_row,
-    out_ref,
     masked,
     ybuf,
     relay,
@@ -62,7 +68,7 @@
     h, j = g // NJ, g % NJ
     y, c = j // NC, j % NC
     z = h * NZL + zl
-    pairs = amp_ref.shape[0] // NJ
+    pairs = amp_hbm.shape[1]
     q = pairs // CHUNKS
     half_cols = NJ * 128
 
@@ -83,47 +89,49 @@
     for peer in peers:
         pl.semaphore_signal(barrier, inc=1, device_id=peer, device_id_type=MESH)
 
+    first, rest = pl.ds(0, q), pl.ds(q, pairs - q)
     loads = [
-        pltpu.make_async_copy(amp_ref, masked, in_sem.at[0]),
-        pltpu.make_async_copy(
-            int_ref.at[:, pl.ds(pl.multiple_of(j * 256, 128), 256)], bline.at[zl], in_sem.at[1]
-        ),
+        pltpu.make_async_copy(src, dst, in_sem.at[i])
+        for i, (src, dst) in enumerate(
+            [
+                (amp_map_hbm, amp_map_ref),
+                (amp_hbm.at[:, first], masked.at[:, first]),
+                (int_map_hbm, int_map_ref),
+                (int_hbm.at[:, pl.ds(pl.multiple_of(j * 256, 128), 256)], bline.at[zl]),
+                (amp_hbm.at[:, rest], masked.at[:, rest]),
+                (pair_hbm, pair_ref),
+                (occ_hbm, occ_ref),
+                (ve_hbm, ve_smem),
+                (ve_row_hbm, ve_row),
+            ]
+        )
     ]
     for load in loads:
         load.start()
 
-    @pl.loop(0, TILE)
-    def _(r):
-        erow[pl.ds(r, 1), :] = jnp.full((1, 128), ve_smem[b * TILE + r], jnp.float32)
-
     lane = lax.broadcasted_iota(jnp.int32, (1, 128), 1)
-    keep0 = amp_map_ref[0, 0].astype(jnp.float32)
-    keep1 = amp_map_ref[0, 1].astype(jnp.float32)
-    amp_mask = jnp.where(lane < TILE, keep0, keep1).astype(jnp.bfloat16)
+
+    def lane_mask(left, right):
+        left, right = left.astype(jnp.float32), right.astype(jnp.float32)
+        return jnp.where(lane < TILE, left, right).astype(jnp.bfloat16)
 
     loads[0].wait()
-
-    @pl.loop(0, NJ * pairs)
-    def _(p):
-        masked[p] = masked[p] * amp_mask
-
-    ybuf[:, j] = masked[pl.ds(j * pairs, pairs)].reshape(CHUNKS, q, TILE, 128)
+    amp_mask = lane_mask(amp_map_ref[0, 0], amp_map_ref[0, 1])
+
+    def mask_chunk(k):
+        for p in range(q):
+            masked[:, k * q + p] = masked[:, k * q + p] * amp_mask[None]
+            ybuf[k, j, p] = masked[j, k * q + p]
+
     loads[1].wait()
-    for half in range(2):
-        tile = 4 * j + 2 * half
-        keep0 = int_map_ref[0, tile].astype(jnp.float32)
-        keep1 = int_map_ref[0, tile + 1].astype(jnp.float32)
-        int_mask = jnp.where(lane < TILE, keep0, keep1).astype(jnp.bfloat16)
-        cols = slice(half * 128, half * 128 + 128)
-        bline[zl, :, cols] = bline[zl, :, cols] * int_mask
-
+    mask_chunk(0)
     pl.semaphore_wait(barrier, len(peers))
 
     def send_chunk(k):
         for d in range(1, NJ):
             jj = (j + d) % NJ
             pltpu.make_async_remote_copy(
-                src_ref=masked.at[pl.ds(jj * pairs + k * q, q)],
+                src_ref=masked.at[jj, pl.ds(k * q, q)],
                 dst_ref=ybuf.at[k, j],
                 send_sem=y_send.at[k],
                 recv_sem=y_recv.at[k],
@@ -132,6 +140,13 @@
             ).start()
 
     send_chunk(0)
+    loads[2].wait()
+    loads[3].wait()
+    for half in range(2):
+        tile = 4 * j + 2 * half
+        cols = slice(half * 128, half * 128 + 128)
+        int_mask = lane_mask(int_map_ref[0, tile], int_map_ref[0, tile + 1])
+        bline[zl, :, cols] = bline[zl, :, cols] * int_mask
 
     def b_hop(r, way):
         step = 1 if way == 0 else -1
@@ -151,7 +166,9 @@
 
     for way in range(2):
         b_hop(1, way).start()
+    loads[4].wait()
     for k in range(1, AHEAD):
+        mask_chunk(k)
         send_chunk(k)
 
     def legs(k, first):
@@ -288,19 +305,41 @@
             cbuf.at[k, j], out_ref.at[pl.ds(j * pairs + k * q, q)], own_sem.at[k]
         )
 
-    lag1, lag2 = 8, 16
+    def sent(k):
+        for copy in legs(k, False):
+            copy.wait_send()
+        drain(cbuf.at[k, pl.ds(0, NJ - 1)], c_send.at[k])
+        own_copy(k).wait()
+
+    def b_sent():
+        for way in range(2):
+            for r in range(1, 5 - way):
+                b_hop(r, way).wait_send()
+
+        @pl.when(in_half)
+        def _():
+            for d in range(1, NX):
+                drain(bfull.at[y, c, x % 2], bx_send.at[d - 1])
+
+        for d in range(1, NY):
+            drain(bfull.at[y, c], by_send.at[d - 1])
+        for copy in b_core_copies():
+            copy.wait_send()
+
+    lag1, lag2 = 4, 8
 
     @pl.loop(0, CHUNKS + lag2)
     def _(t):
-        @pl.when(t + AHEAD < CHUNKS)
-        def _():
-            send_chunk(t + AHEAD)
-
         @pl.when(t < CHUNKS)
         def _():
             drain(ybuf.at[t, pl.ds(0, NJ - 1)], y_recv.at[t])
             for copy in legs(t, True):
                 copy.start()
+
+        @pl.when(t + AHEAD < CHUNKS)
+        def _():
+            mask_chunk(t + AHEAD)
+            send_chunk(t + AHEAD)
 
         for r in range(1, 4):
 
@@ -314,6 +353,12 @@
         @pl.when(t == 3)
         def _():
             b_along_x()
+            for load in loads[5:]:
+                load.wait()
+
+            @pl.loop(0, TILE)
+            def _(r):
+                erow[pl.ds(r, 1), :] = jnp.full((1, 128), ve_smem[b * TILE + r], jnp.float32)
 
         @pl.when(jnp.logical_and(t >= lag1, t < CHUNKS + lag1))
         def _():
@@ -323,59 +368,44 @@
                 first[way].wait_recv()
                 second[way].start()
 
+        @pl.when(t == 5)
+        def _():
+            b_along_y()
+
         @pl.when(t == 6)
-        def _():
-            b_along_y()
-
-        @pl.when(t == 9)
         def _():
             for copy in b_core():
                 copy.start()
 
-        @pl.when(t == 12)
+        @pl.when(t == lag2)
         def _():
             other = 1 - c
             for yy in range(NY):
                 drain(bfull.at[yy, other], bc_recv.at[yy])
-
-        @pl.when(jnp.logical_and(t >= 12, t < 12 + CHUNKS // GROUP))
-        def _():
-            own_half(t - 12)
+            b_sent()
 
         @pl.when(t >= lag2)
         def _():
             k = t - lag2
+
+            @pl.when(k % GROUP == 0)
+            def _():
+                own_half(k // GROUP)
+
+            drain(ybuf.at[k, pl.ds(0, NJ - 1)], y_send.at[k])
+            for copy in legs(k, True):
+                copy.wait_send()
+
+            @pl.when(k > 0)
+            def _():
+                sent(k - 1)
+
             for copy in legs(k, False):
                 copy.wait_recv()
             compute(k)
 
+    sent(CHUNKS - 1)
     drain(out_ref.at[pl.ds(0, (NJ - 1) * pairs)], c_recv)
-
-    @pl.loop(0, CHUNKS)
-    def _(k):
-        drain(ybuf.at[k, pl.ds(0, NJ - 1)], y_send.at[k])
-        for copy in legs(k, True) + legs(k, False):
-            copy.wait_send()
-        drain(cbuf.at[k, pl.ds(0, NJ - 1)], c_send.at[k])
-        own_copy(k).wait()
-
-    for way in range(2):
-        for r in range(1, 5 - way):
-            b_hop(r, way).wait_send()
-
-    @pl.when(in_half)
-    def _():
-        for d in range(1, NX):
-            drain(bfull.at[y, c, x % 2], bx_send.at[d - 1])
-
-    for d in range(1, NY):
-        drain(bfull.at[y, c], by_send.at[d - 1])
-    for copy in b_core_copies():
-        copy.wait_send()
-
-
-def copy_out(src_ref, dst_ref):
-    dst_ref[...] = src_ref[...]
 
 
 def body(
@@ -383,18 +413,22 @@
 ):
     pair_count, rows, cols = amplitudes.shape
     q = pair_count // NJ // CHUNKS
-    vmem = pl.BlockSpec(memory_space=pltpu.VMEM)
     hbm = pl.BlockSpec(memory_space=pl.ANY)
-    smem = pl.BlockSpec(memory_space=pltpu.SMEM)
     dma = pltpu.SemaphoreType.DMA
     block = pltpu.VMEM((CHUNKS, NJ, q, rows, cols), jnp.bfloat16)
-    update = pl.pallas_call(
+    return pl.pallas_call(
         kernel,
         out_shape=jax.ShapeDtypeStruct(amplitudes.shape, jnp.bfloat16),
-        in_specs=[hbm, smem, hbm, smem, smem, smem, smem, vmem],
+        in_specs=[hbm] * 8,
         out_specs=pl.BlockSpec(memory_space=pl.ANY),
         scratch_shapes=[
-            pltpu.VMEM(amplitudes.shape, jnp.bfloat16),
+            pltpu.SMEM(amplitude_map.shape, jnp.int32),
+            pltpu.SMEM(integral_map.shape, jnp.int32),
+            pltpu.SMEM((2, pair_count), jnp.int32),
+            pltpu.SMEM(occupied_energy.shape, jnp.float32),
+            pltpu.SMEM(virtual_energy.shape, jnp.float32),
+            pltpu.VMEM((1, virtual_energy.size), jnp.float32),
+            pltpu.VMEM((NJ, pair_count // NJ, rows, cols), jnp.bfloat16),
             block,
             block,
             block,
@@ -420,7 +454,7 @@
             dma((NY,)),
             dma((NY,)),
             dma((NY,)),
-            dma((2,)),
+            dma((9,)),
         ],
         compiler_params=pltpu.CompilerParams(
             collective_id=0, has_side_effects=True, vmem_limit_bytes=60 * 1024 * 1024
@@ -429,7 +463,7 @@
             flops=2 * 1024 * 2048 * 1024, bytes_accessed=8 * 1024 * 1024, transcendentals=0
         ),
     )(
-        amplitudes,
+        amplitudes.reshape(NJ, pair_count // NJ, rows, cols),
         amplitude_map,
         integrals,
         integral_map,
@@ -438,15 +472,6 @@
         virtual_energy,
         virtual_energy.reshape(1, -1),
     )
-    part = pl.BlockSpec((pair_count // 8, rows, cols), lambda i: (i, 0, 0))
-    return pl.pallas_call(
-        copy_out,
-        grid=(8,),
-        out_shape=jax.ShapeDtypeStruct(amplitudes.shape, jnp.bfloat16),
-        in_specs=[part],
-        out_specs=part,
-        compiler_params=pltpu.CompilerParams(vmem_limit_bytes=60 * 1024 * 1024),
-    )(update)
 
 
 def solution(mesh):

time: 218 us -> 216 us (level)
  Pallas kernels: 218 us -> 212 us
  local copies, waits for them, and re-layouts: 0 us -> 3.08 us
    pallas_call x1 -> x0, Pallas kernels: 5.64 us -> none  [body(): pl.pallas_call(copy_out, grid=(8,), out_shape=jax.ShapeDtypeStruct(amplit...]
    unnamed x0 -> x1, local copies, waits for them, and re-layouts: none -> 3.08 us
where the time goes in v5:
time: 216 us; the launch traced here: 215 us
  Pallas kernels  212 us (98%)
  local copies, waits for them, and re-layouts  3.08 us (1%)
    pallas_call x1, Pallas kernels, body(): pl.pallas_call(kernel, out_shape=jax.ShapeDtypeStruct(amplitudes.shape, j...  212 us

profile of v5, /device:TPU:1, one launch (start us, length us, event | category | flops | bytes accessed | tf_op | source)
XLA Modules:
  0.0 214.6 jit_solution(15579998634184099911)
XLA Ops:
  0.0 211.5 %shard_map.73 = bf16[128,64,128]{2,1,0:T(8,128)(2,1)} custom-call(bf16[8,16,64,128]{3,2,1,0:T(8,128)(2,1)} %bitcast.3, s32[1,2]{1,0:T(1,128)} %amp_map_hbm.1, bf16[64,2048]{1,0:T(8,128)(2,1)} %int_hbm.1, s32[1,32]{1,0:T(1,128)} %int_map_hbm.1, s32[2,128]{1,0:T(2,128)} %bitcast.5, f32[128]{0:T(128)} %occ_hbm.1, f32[2048]{0:T(1024)} %ve_hbm.1, f32[1,2048]{1,0:T(1,128)} %bitcast.4), custom_call_target="tpu_custom_call" | custom-call | flops 4294967296 | bytes 8388608 | tf_op jit(solution)/shard_map/pallas_call | solution.py:419
  211.5 3.1 %copy.9 = bf16[128,64,128]{2,1,0:T(8,128)(2,1)} copy(bf16[128,64,128]{2,1,0:T(8,128)(2,1)} %shard_map.73) | data formatting | bytes 4194304

commit v6 on v5

--- a/solution.py
+++ b/solution.py
@@ -177,14 +177,13 @@
         ssem, rsem = (z_send, z_recv) if first else (f_send, f_recv)
         return [
             pltpu.make_async_remote_copy(
-                src_ref=src.at[k, pl.ds(4 * way, 4)],
-                dst_ref=dst.at[k, pl.ds(4 * way, 4)],
-                send_sem=ssem.at[k, way],
-                recv_sem=rsem.at[k, way],
-                device_id=at_z(z + (hops if way == 0 else -hops)),
+                src_ref=src.at[k],
+                dst_ref=dst.at[k],
+                send_sem=ssem.at[k],
+                recv_sem=rsem.at[k],
+                device_id=at_z(z + hops * (1 - 2 * c)),
                 device_id_type=MESH,
             )
-            for way in range(2)
         ]
 
     in_half = x // 2 == h
@@ -363,10 +362,9 @@
         @pl.when(jnp.logical_and(t >= lag1, t < CHUNKS + lag1))
         def _():
             k = t - lag1
-            first, second = legs(k, True), legs(k, False)
-            for way in range(2):
-                first[way].wait_recv()
-                second[way].start()
+            for first, second in zip(legs(k, True), legs(k, False)):
+                first.wait_recv()
+                second.start()
 
         @pl.when(t == 5)
         def _():
@@ -439,10 +437,10 @@
             pltpu.VMEM((TILE, 128), jnp.float32),
             dma((CHUNKS,)),
             dma((CHUNKS,)),
-            dma((CHUNKS, 2)),
-            dma((CHUNKS, 2)),
-            dma((CHUNKS, 2)),
-            dma((CHUNKS, 2)),
+            dma((CHUNKS,)),
+            dma((CHUNKS,)),
+            dma((CHUNKS,)),
+            dma((CHUNKS,)),
             dma((CHUNKS,)),
             dma,
             dma((CHUNKS,)),

time: 216 us -> 215 us (level)
  no operation moved by 1% of the time
where the time goes in v6:
time: 215 us; the launch traced here: 213 us
  Pallas kernels  210 us (98%)
  local copies, waits for them, and re-layouts  3.08 us (1%)
    pallas_call x1, Pallas kernels, body(): pl.pallas_call(kernel, out_shape=jax.ShapeDtypeStruct(amplitudes.shape, j...  210 us

profile of v6, /device:TPU:1, one launch (start us, length us, event | category | flops | bytes accessed | tf_op | source)
XLA Modules:
  0.0 213.0 jit_solution(7923651816013982382)
XLA Ops:
  0.0 209.9 %shard_map.73 = bf16[128,64,128]{2,1,0:T(8,128)(2,1)} custom-call(bf16[8,16,64,128]{3,2,1,0:T(8,128)(2,1)} %bitcast.3, s32[1,2]{1,0:T(1,128)} %amp_map_hbm.1, bf16[64,2048]{1,0:T(8,128)(2,1)} %int_hbm.1, s32[1,32]{1,0:T(1,128)} %int_map_hbm.1, s32[2,128]{1,0:T(2,128)} %bitcast.5, f32[128]{0:T(128)} %occ_hbm.1, f32[2048]{0:T(1024)} %ve_hbm.1, f32[1,2048]{1,0:T(1,128)} %bitcast.4), custom_call_target="tpu_custom_call" | custom-call | flops 4294967296 | bytes 8388608 | tf_op jit(solution)/shard_map/pallas_call | solution.py:417
  209.9 3.1 %copy.9 = bf16[128,64,128]{2,1,0:T(8,128)(2,1)} copy(bf16[128,64,128]{2,1,0:T(8,128)(2,1)} %shard_map.73) | data formatting | bytes 4194304

commit v7 on v6

--- a/solution.py
+++ b/solution.py
@@ -325,7 +325,20 @@
         for copy in b_core_copies():
             copy.wait_send()
 
-    lag1, lag2 = 4, 8
+    def finish(k):
+        drain(ybuf.at[k, pl.ds(0, NJ - 1)], y_send.at[k])
+        for copy in legs(k, True):
+            copy.wait_send()
+
+        @pl.when(k > 0)
+        def _():
+            sent(k - 1)
+
+        for copy in legs(k, False):
+            copy.wait_recv()
+        compute(k)
+
+    lag1, lag2, start = 4, 8, 12
 
     @pl.loop(0, CHUNKS + lag2)
     def _(t):
@@ -335,21 +348,31 @@
             for copy in legs(t, True):
                 copy.start()
 
-        @pl.when(t + AHEAD < CHUNKS)
-        def _():
-            mask_chunk(t + AHEAD)
-            send_chunk(t + AHEAD)
+        for e in range(2):
+            ahead = AHEAD + 2 * t + e
+
+            @pl.when(ahead < CHUNKS)
+            def _():
+                mask_chunk(ahead)
+                send_chunk(ahead)
+
+        @pl.when(jnp.logical_and(t >= lag1, t < CHUNKS + lag1))
+        def _():
+            k = t - lag1
+            for first, second in zip(legs(k, True), legs(k, False)):
+                first.wait_recv()
+                second.start()
 
         for r in range(1, 4):
 
-            @pl.when(t == r - 1)
+            @pl.when(t == lag1 + r - 1)
             def _():
                 for way in range(2):
                     b_arrived(r, way)
                     if r + way < 4:
                         b_hop(r + 1, way).start()
 
-        @pl.when(t == 3)
+        @pl.when(t == 7)
         def _():
             b_along_x()
             for load in loads[5:]:
@@ -359,48 +382,34 @@
             def _(r):
                 erow[pl.ds(r, 1), :] = jnp.full((1, 128), ve_smem[b * TILE + r], jnp.float32)
 
-        @pl.when(jnp.logical_and(t >= lag1, t < CHUNKS + lag1))
-        def _():
-            k = t - lag1
-            for first, second in zip(legs(k, True), legs(k, False)):
-                first.wait_recv()
-                second.start()
-
-        @pl.when(t == 5)
+        @pl.when(t == 9)
         def _():
             b_along_y()
 
-        @pl.when(t == 6)
+        @pl.when(t == 11)
         def _():
             for copy in b_core():
                 copy.start()
 
-        @pl.when(t == lag2)
+        @pl.when(t == start)
         def _():
             other = 1 - c
             for yy in range(NY):
                 drain(bfull.at[yy, other], bc_recv.at[yy])
             b_sent()
 
-        @pl.when(t >= lag2)
-        def _():
-            k = t - lag2
-
-            @pl.when(k % GROUP == 0)
-            def _():
-                own_half(k // GROUP)
-
-            drain(ybuf.at[k, pl.ds(0, NJ - 1)], y_send.at[k])
-            for copy in legs(k, True):
-                copy.wait_send()
-
-            @pl.when(k > 0)
-            def _():
-                sent(k - 1)
-
-            for copy in legs(k, False):
-                copy.wait_recv()
-            compute(k)
+        @pl.when(jnp.logical_and(t >= start, t < start + CHUNKS // GROUP))
+        def _():
+            own_half(t - start)
+
+        @pl.when(jnp.logical_and(t >= start, t < 2 * start - lag2))
+        def _():
+            for e in range(2):
+                finish(2 * (t - start) + e)
+
+        @pl.when(t >= 2 * start - lag2)
+        def _():
+            finish(t - lag2)
 
     sent(CHUNKS - 1)
     drain(out_ref.at[pl.ds(0, (NJ - 1) * pairs)], c_recv)

time: 215 us -> 215 us (level)
  no operation moved by 1% of the time
where the time goes in v7:
time: 215 us
  Pallas kernels  212 us (99%)
  local copies, waits for them, and re-layouts  3.08 us (1%)
    pallas_call x1, Pallas kernels, body(): pl.pallas_call(kernel, out_shape=jax.ShapeDtypeStruct(amplitudes.shape, j...  212 us

profile of v7, /device:TPU:1, one launch (start us, length us, event | category | flops | bytes accessed | tf_op | source)
XLA Modules:
  0.0 215.1 jit_solution(11338235269807066442)
XLA Ops:
  0.0 212.0 %shard_map.73 = bf16[128,64,128]{2,1,0:T(8,128)(2,1)} custom-call(bf16[8,16,64,128]{3,2,1,0:T(8,128)(2,1)} %bitcast.3, s32[1,2]{1,0:T(1,128)} %amp_map_hbm.1, bf16[64,2048]{1,0:T(8,128)(2,1)} %int_hbm.1, s32[1,32]{1,0:T(1,128)} %int_map_hbm.1, s32[2,128]{1,0:T(2,128)} %bitcast.5, f32[128]{0:T(128)} %occ_hbm.1, f32[2048]{0:T(1024)} %ve_hbm.1, f32[1,2048]{1,0:T(1,128)} %bitcast.4), custom_call_target="tpu_custom_call" | custom-call | flops 4294967296 | bytes 8388608 | tf_op jit(solution)/shard_map/pallas_call | solution.py:426
  212.0 3.1 %copy.9 = bf16[128,64,128]{2,1,0:T(8,128)(2,1)} copy(bf16[128,64,128]{2,1,0:T(8,128)(2,1)} %shard_map.73) | data formatting | bytes 4194304

commit v8 on v7

--- a/solution.py
+++ b/solution.py
@@ -61,6 +61,8 @@
     bc_send,
     bc_recv,
     in_sem,
+    hand_send,
+    hand_recv,
 ):
     b = lax.axis_index("blk")
     g = lax.axis_index("grp")
@@ -139,6 +141,46 @@
                 device_id_type=MESH,
             ).start()
 
+    def legs(k, first):
+        slot = (k + CHUNKS - 1) % CHUNKS + 1
+        src, dst = (ybuf, relay) if first else (relay, zbuf)
+        hops = LEGS[0] if first else LEGS[1]
+        ssem, rsem = (z_send, z_recv) if first else (f_send, f_recv)
+        return [
+            pltpu.make_async_remote_copy(
+                src_ref=src.at[k],
+                dst_ref=dst.at[k if first else slot],
+                send_sem=ssem.at[k],
+                recv_sem=rsem.at[k],
+                device_id=at_z(z + hops * (1 - 2 * c)),
+                device_id_type=MESH,
+            )
+        ]
+
+    def head_leg():
+        return pltpu.make_async_remote_copy(
+            src_ref=masked.at[:, pl.ds(0, q)],
+            dst_ref=relay.at[0],
+            send_sem=z_send.at[0],
+            recv_sem=z_recv.at[0],
+            device_id=at_z(z + LEGS[0] * (1 - 2 * c)),
+            device_id_type=MESH,
+        )
+
+    def hand_on():
+        for d in range(1, NJ):
+            jj = (j + d) % NJ
+            pltpu.make_async_remote_copy(
+                src_ref=zbuf.at[CHUNKS, jj],
+                dst_ref=zbuf.at[0, j],
+                send_sem=hand_send,
+                recv_sem=hand_recv,
+                device_id=at_j(jj),
+                device_id_type=MESH,
+            ).start()
+        zbuf[0, j] = zbuf[CHUNKS, j]
+
+    head_leg().start()
     send_chunk(0)
     loads[2].wait()
     loads[3].wait()
@@ -170,21 +212,6 @@
     for k in range(1, AHEAD):
         mask_chunk(k)
         send_chunk(k)
-
-    def legs(k, first):
-        src, dst = (ybuf, relay) if first else (relay, zbuf)
-        hops = LEGS[0] if first else LEGS[1]
-        ssem, rsem = (z_send, z_recv) if first else (f_send, f_recv)
-        return [
-            pltpu.make_async_remote_copy(
-                src_ref=src.at[k],
-                dst_ref=dst.at[k],
-                send_sem=ssem.at[k],
-                recv_sem=rsem.at[k],
-                device_id=at_z(z + hops * (1 - 2 * c)),
-                device_id_type=MESH,
-            )
-        ]
 
     in_half = x // 2 == h
 
@@ -334,8 +361,11 @@
         def _():
             sent(k - 1)
 
-        for copy in legs(k, False):
-            copy.wait_recv()
+        @pl.when(k > 0)
+        def _():
+            for copy in legs(k, False):
+                copy.wait_recv()
+
         compute(k)
 
     lag1, lag2, start = 4, 8, 12
@@ -345,8 +375,11 @@
         @pl.when(t < CHUNKS)
         def _():
             drain(ybuf.at[t, pl.ds(0, NJ - 1)], y_recv.at[t])
-            for copy in legs(t, True):
-                copy.start()
+
+            @pl.when(t > 0)
+            def _():
+                for copy in legs(t, True):
+                    copy.start()
 
         for e in range(2):
             ahead = AHEAD + 2 * t + e
@@ -382,6 +415,12 @@
             def _(r):
                 erow[pl.ds(r, 1), :] = jnp.full((1, 128), ve_smem[b * TILE + r], jnp.float32)
 
+        @pl.when(t == lag2)
+        def _():
+            for copy in legs(0, False):
+                copy.wait_recv()
+            hand_on()
+
         @pl.when(t == 9)
         def _():
             b_along_y()
@@ -397,6 +436,8 @@
             for yy in range(NY):
                 drain(bfull.at[yy, other], bc_recv.at[yy])
             b_sent()
+            drain(zbuf.at[0, pl.ds(0, NJ - 1)], hand_recv)
+            drain(zbuf.at[0, pl.ds(0, NJ - 1)], hand_send)
 
         @pl.when(jnp.logical_and(t >= start, t < start + CHUNKS // GROUP))
         def _():
@@ -438,7 +479,7 @@
             pltpu.VMEM((NJ, pair_count // NJ, rows, cols), jnp.bfloat16),
             block,
             block,
-            block,
+            pltpu.VMEM((CHUNKS + 1, NJ, q, rows, cols), jnp.bfloat16),
             block,
             pltpu.VMEM((NZL, TILE, 256), jnp.bfloat16),
             pltpu.VMEM((NY, NC, 2, 256, NZL * TILE), jnp.bfloat16),
@@ -462,6 +503,8 @@
             dma((NY,)),
             dma((NY,)),
             dma((9,)),
+            dma,
+            dma,
         ],
         compiler_params=pltpu.CompilerParams(
             collective_id=0, has_side_effects=True, vmem_limit_bytes=60 * 1024 * 1024

time: 215 us -> 211 us (0.981)
  Pallas kernels: 212 us -> 207 us
    pallas_call x1, Pallas kernels: 212 us -> 207 us  [body(): pl.pallas_call(kernel, out_shape=jax.ShapeDtypeStruct(amplitudes.shape, j...]
where the time goes in v8:
time: 211 us; the launch traced here: 210 us
  Pallas kernels  207 us (98%)
  local copies, waits for them, and re-layouts  3.08 us (1%)
    pallas_call x1, Pallas kernels, body(): pl.pallas_call(kernel, out_shape=jax.ShapeDtypeStruct(amplitudes.shape, j...  207 us

profile of v8, /device:TPU:1, one launch (start us, length us, event | category | flops | bytes accessed | tf_op | source)
XLA Modules:
  0.0 210.4 jit_solution(7071535961068042561)
XLA Ops:
  0.0 207.3 %shard_map.73 = bf16[128,64,128]{2,1,0:T(8,128)(2,1)} custom-call(bf16[8,16,64,128]{3,2,1,0:T(8,128)(2,1)} %bitcast.3, s32[1,2]{1,0:T(1,128)} %amp_map_hbm.1, bf16[64,2048]{1,0:T(8,128)(2,1)} %int_hbm.1, s32[1,32]{1,0:T(1,128)} %int_map_hbm.1, s32[2,128]{1,0:T(2,128)} %bitcast.5, f32[128]{0:T(128)} %occ_hbm.1, f32[2048]{0:T(1024)} %ve_hbm.1, f32[1,2048]{1,0:T(1,128)} %bitcast.4), custom_call_target="tpu_custom_call" | custom-call | flops 4294967296 | bytes 8388608 | tf_op jit(solution)/shard_map/pallas_call | solution.py:467
  207.3 3.1 %copy.9 = bf16[128,64,128]{2,1,0:T(8,128)(2,1)} copy(bf16[128,64,128]{2,1,0:T(8,128)(2,1)} %shard_map.73) | data formatting | bytes 4194304

commit v9 on v8

--- a/solution.py
+++ b/solution.py
@@ -9,7 +9,7 @@
 TILE = 64
 NX, NZ, NZL, NJ, NY, NC = 4, 16, 8, 8, 4, 2
 CHUNKS = 16
-AHEAD = 2
+HEAD, AHEAD = 2, 4
 GROUP = 4
 LEGS = (5, 3)
 
@@ -91,7 +91,7 @@
     for peer in peers:
         pl.semaphore_signal(barrier, inc=1, device_id=peer, device_id_type=MESH)
 
-    first, rest = pl.ds(0, q), pl.ds(q, pairs - q)
+    first, rest = pl.ds(0, HEAD * q), pl.ds(HEAD * q, pairs - HEAD * q)
     loads = [
         pltpu.make_async_copy(src, dst, in_sem.at[i])
         for i, (src, dst) in enumerate(
@@ -126,7 +126,8 @@
             ybuf[k, j, p] = masked[j, k * q + p]
 
     loads[1].wait()
-    mask_chunk(0)
+    for k in range(HEAD):
+        mask_chunk(k)
     pl.semaphore_wait(barrier, len(peers))
 
     def send_chunk(k):
@@ -142,7 +143,7 @@
             ).start()
 
     def legs(k, first):
-        slot = (k + CHUNKS - 1) % CHUNKS + 1
+        slot = (k + CHUNKS - HEAD) % CHUNKS + HEAD
         src, dst = (ybuf, relay) if first else (relay, zbuf)
         hops = LEGS[0] if first else LEGS[1]
         ssem, rsem = (z_send, z_recv) if first else (f_send, f_recv)
@@ -157,31 +158,34 @@
             )
         ]
 
-    def head_leg():
+    def head_leg(k):
         return pltpu.make_async_remote_copy(
-            src_ref=masked.at[:, pl.ds(0, q)],
-            dst_ref=relay.at[0],
-            send_sem=z_send.at[0],
-            recv_sem=z_recv.at[0],
+            src_ref=masked.at[:, pl.ds(k * q, q)],
+            dst_ref=relay.at[k],
+            send_sem=z_send.at[k],
+            recv_sem=z_recv.at[k],
             device_id=at_z(z + LEGS[0] * (1 - 2 * c)),
             device_id_type=MESH,
         )
 
-    def hand_on():
+    def hand_on(k):
         for d in range(1, NJ):
             jj = (j + d) % NJ
             pltpu.make_async_remote_copy(
-                src_ref=zbuf.at[CHUNKS, jj],
-                dst_ref=zbuf.at[0, j],
-                send_sem=hand_send,
-                recv_sem=hand_recv,
+                src_ref=zbuf.at[CHUNKS + k, jj],
+                dst_ref=zbuf.at[k, j],
+                send_sem=hand_send.at[k],
+                recv_sem=hand_recv.at[k],
                 device_id=at_j(jj),
                 device_id_type=MESH,
             ).start()
-        zbuf[0, j] = zbuf[CHUNKS, j]
-
-    head_leg().start()
-    send_chunk(0)
+        zbuf[k, j] = zbuf[CHUNKS + k, j]
+
+    for k in range(HEAD):
+        head_leg(k).start()
+    loads[4].wait()
+    mask_chunk(HEAD)
+    send_chunk(HEAD)
     loads[2].wait()
     loads[3].wait()
     for half in range(2):
@@ -208,8 +212,7 @@
 
     for way in range(2):
         b_hop(1, way).start()
-    loads[4].wait()
-    for k in range(1, AHEAD):
+    for k in range(HEAD + 1, AHEAD):
         mask_chunk(k)
         send_chunk(k)
 
@@ -361,7 +364,7 @@
         def _():
             sent(k - 1)
 
-        @pl.when(k > 0)
+        @pl.when(k >= HEAD)
         def _():
             for copy in legs(k, False):
                 copy.wait_recv()
@@ -372,14 +375,11 @@
 
     @pl.loop(0, CHUNKS + lag2)
     def _(t):
-        @pl.when(t < CHUNKS)
+        @pl.when(jnp.logical_and(t >= HEAD, t < CHUNKS))
         def _():
             drain(ybuf.at[t, pl.ds(0, NJ - 1)], y_recv.at[t])
-
-            @pl.when(t > 0)
-            def _():
-                for copy in legs(t, True):
-                    copy.start()
+            for copy in legs(t, True):
+                copy.start()
 
         for e in range(2):
             ahead = AHEAD + 2 * t + e
@@ -395,6 +395,11 @@
             for first, second in zip(legs(k, True), legs(k, False)):
                 first.wait_recv()
                 second.start()
+
+        @pl.when(t == 7)
+        def _():
+            for k in range(HEAD):
+                send_chunk(k)
 
         for r in range(1, 4):
 
@@ -415,11 +420,11 @@
             def _(r):
                 erow[pl.ds(r, 1), :] = jnp.full((1, 128), ve_smem[b * TILE + r], jnp.float32)
 
-        @pl.when(t == lag2)
-        def _():
-            for copy in legs(0, False):
+        @pl.when(jnp.logical_and(t >= lag2, t < lag2 + HEAD))
+        def _():
+            for copy in legs(t - lag2, False):
                 copy.wait_recv()
-            hand_on()
+            hand_on(t - lag2)
 
         @pl.when(t == 9)
         def _():
@@ -436,8 +441,10 @@
             for yy in range(NY):
                 drain(bfull.at[yy, other], bc_recv.at[yy])
             b_sent()
-            drain(zbuf.at[0, pl.ds(0, NJ - 1)], hand_recv)
-            drain(zbuf.at[0, pl.ds(0, NJ - 1)], hand_send)
+            for k in range(HEAD):
+                drain(ybuf.at[k, pl.ds(0, NJ - 1)], y_recv.at[k])
+                drain(zbuf.at[k, pl.ds(0, NJ - 1)], hand_recv.at[k])
+                drain(zbuf.at[k, pl.ds(0, NJ - 1)], hand_send.at[k])
 
         @pl.when(jnp.logical_and(t >= start, t < start + CHUNKS // GROUP))
         def _():
@@ -479,7 +486,7 @@
             pltpu.VMEM((NJ, pair_count // NJ, rows, cols), jnp.bfloat16),
             block,
             block,
-            pltpu.VMEM((CHUNKS + 1, NJ, q, rows, cols), jnp.bfloat16),
+            pltpu.VMEM((CHUNKS + HEAD, NJ, q, rows, cols), jnp.bfloat16),
             block,
             pltpu.VMEM((NZL, TILE, 256), jnp.bfloat16),
             pltpu.VMEM((NY, NC, 2, 256, NZL * TILE), jnp.bfloat16),
@@ -503,8 +510,8 @@
             dma((NY,)),
             dma((NY,)),
             dma((9,)),
-            dma,
-            dma,
+            dma((HEAD,)),
+            dma((HEAD,)),
         ],
         compiler_params=pltpu.CompilerParams(
             collective_id=0, has_side_effects=True, vmem_limit_bytes=60 * 1024 * 1024

time: 211 us -> 211 us (level)
  no operation moved by 1% of the time
where the time goes in v9:
time: 211 us; the launch traced here: 210 us
  Pallas kernels  207 us (98%)
  local copies, waits for them, and re-layouts  3.08 us (1%)
    pallas_call x1, Pallas kernels, body(): pl.pallas_call(kernel, out_shape=jax.ShapeDtypeStruct(amplitudes.shape, j...  207 us

profile of v9, /device:TPU:1, one launch (start us, length us, event | category | flops | bytes accessed | tf_op | source)
XLA Modules:
  0.0 210.4 jit_solution(4187241418124153834)
XLA Ops:
  0.0 207.3 %shard_map.73 = bf16[128,64,128]{2,1,0:T(8,128)(2,1)} custom-call(bf16[8,16,64,128]{3,2,1,0:T(8,128)(2,1)} %bitcast.3, s32[1,2]{1,0:T(1,128)} %amp_map_hbm.1, bf16[64,2048]{1,0:T(8,128)(2,1)} %int_hbm.1, s32[1,32]{1,0:T(1,128)} %int_map_hbm.1, s32[2,128]{1,0:T(2,128)} %bitcast.5, f32[128]{0:T(128)} %occ_hbm.1, f32[2048]{0:T(1024)} %ve_hbm.1, f32[1,2048]{1,0:T(1,128)} %bitcast.4), custom_call_target="tpu_custom_call" | custom-call | flops 4294967296 | bytes 8388608 | tf_op jit(solution)/shard_map/pallas_call | solution.py:474
  207.3 3.1 %copy.9 = bf16[128,64,128]{2,1,0:T(8,128)(2,1)} copy(bf16[128,64,128]{2,1,0:T(8,128)(2,1)} %shard_map.73) | data formatting | bytes 4194304

commit v10 on v9

--- a/solution.py
+++ b/solution.py
@@ -142,21 +142,26 @@
                 device_id_type=MESH,
             ).start()
 
-    def legs(k, first):
+    def first_leg(k):
+        return pltpu.make_async_remote_copy(
+            src_ref=ybuf.at[k],
+            dst_ref=relay.at[k],
+            send_sem=z_send.at[k],
+            recv_sem=z_recv.at[k],
+            device_id=at_z(z + LEGS[0] * (1 - 2 * c)),
+            device_id_type=MESH,
+        )
+
+    def second_leg(k, part):
         slot = (k + CHUNKS - HEAD) % CHUNKS + HEAD
-        src, dst = (ybuf, relay) if first else (relay, zbuf)
-        hops = LEGS[0] if first else LEGS[1]
-        ssem, rsem = (z_send, z_recv) if first else (f_send, f_recv)
-        return [
-            pltpu.make_async_remote_copy(
-                src_ref=src.at[k],
-                dst_ref=dst.at[k if first else slot],
-                send_sem=ssem.at[k],
-                recv_sem=rsem.at[k],
-                device_id=at_z(z + hops * (1 - 2 * c)),
-                device_id_type=MESH,
-            )
-        ]
+        return pltpu.make_async_remote_copy(
+            src_ref=relay.at[k, pl.ds(4 * part, 4)],
+            dst_ref=zbuf.at[slot, pl.ds(4 * part, 4)],
+            send_sem=f_send.at[k, part],
+            recv_sem=f_recv.at[k, part],
+            device_id=at_z(z + LEGS[1] * (1 - 2 * c)),
+            device_id_type=MESH,
+        )
 
     def head_leg(k):
         return pltpu.make_async_remote_copy(
@@ -292,12 +297,24 @@
                 )
             own_acc[n, pl.ds(group * GROUP, GROUP)] = acc.reshape(GROUP, q * TILE, 256)
 
+    def half_product(k):
+        @pl.loop(0, 4)
+        def _(n):
+            acc = own_acc[n, k]
+            for i in range(2):
+                acc += jnp.dot(
+                    rows_of(zbuf, k, 1, i),
+                    weights(1 - h, i, n),
+                    preferred_element_type=jnp.float32,
+                )
+            own_acc[n, k] = acc
+
     def compute(k):
         @pl.loop(0, 4)
         def _(step):
             n = (step + y) % 4
             acc = own_acc[n, k]
-            for i in range(4):
+            for i in range(2, 4):
                 acc += jnp.dot(
                     rows_of(zbuf, k, 1, i),
                     weights(1 - h, i, n),
@@ -335,8 +352,8 @@
         )
 
     def sent(k):
-        for copy in legs(k, False):
-            copy.wait_send()
+        for part in range(2):
+            second_leg(k, part).wait_send()
         drain(cbuf.at[k, pl.ds(0, NJ - 1)], c_send.at[k])
         own_copy(k).wait()
 
@@ -357,18 +374,20 @@
 
     def finish(k):
         drain(ybuf.at[k, pl.ds(0, NJ - 1)], y_send.at[k])
-        for copy in legs(k, True):
-            copy.wait_send()
+        first_leg(k).wait_send()
 
         @pl.when(k > 0)
         def _():
             sent(k - 1)
 
-        @pl.when(k >= HEAD)
-        def _():
-            for copy in legs(k, False):
-                copy.wait_recv()
-
+        for part in range(2):
+
+            @pl.when(k >= HEAD)
+            def _():
+                second_leg(k, part).wait_recv()
+
+            if part == 0:
+                half_product(k)
         compute(k)
 
     lag1, lag2, start = 4, 8, 12
@@ -378,8 +397,7 @@
         @pl.when(jnp.logical_and(t >= HEAD, t < CHUNKS))
         def _():
             drain(ybuf.at[t, pl.ds(0, NJ - 1)], y_recv.at[t])
-            for copy in legs(t, True):
-                copy.start()
+            first_leg(t).start()
 
         for e in range(2):
             ahead = AHEAD + 2 * t + e
@@ -392,9 +410,9 @@
         @pl.when(jnp.logical_and(t >= lag1, t < CHUNKS + lag1))
         def _():
             k = t - lag1
-            for first, second in zip(legs(k, True), legs(k, False)):
-                first.wait_recv()
-                second.start()
+            first_leg(k).wait_recv()
+            for part in range(2):
+                second_leg(k, part).start()
 
         @pl.when(t == 7)
         def _():
@@ -422,8 +440,8 @@
 
         @pl.when(jnp.logical_and(t >= lag2, t < lag2 + HEAD))
         def _():
-            for copy in legs(t - lag2, False):
-                copy.wait_recv()
+            for part in range(2):
+                second_leg(t - lag2, part).wait_recv()
             hand_on(t - lag2)
 
         @pl.when(t == 9)
@@ -496,8 +514,8 @@
             dma((CHUNKS,)),
             dma((CHUNKS,)),
             dma((CHUNKS,)),
-            dma((CHUNKS,)),
-            dma((CHUNKS,)),
+            dma((CHUNKS, 2)),
+            dma((CHUNKS, 2)),
             dma((CHUNKS,)),
             dma,
             dma((CHUNKS,)),

time: 211 us -> 212 us (level)
  no operation moved by 1% of the time
where the time goes in v10:
time: 212 us
  Pallas kernels  209 us (99%)
  local copies, waits for them, and re-layouts  3.08 us (1%)
    pallas_call x1, Pallas kernels, body(): pl.pallas_call(kernel, out_shape=jax.ShapeDtypeStruct(amplitudes.shape, j...  209 us

profile of v10, /device:TPU:1, one launch (start us, length us, event | category | flops | bytes accessed | tf_op | source)
XLA Modules:
  0.0 211.7 jit_solution(6951528291607623755)
XLA Ops:
  0.0 208.6 %shard_map.73 = bf16[128,64,128]{2,1,0:T(8,128)(2,1)} custom-call(bf16[8,16,64,128]{3,2,1,0:T(8,128)(2,1)} %bitcast.3, s32[1,2]{1,0:T(1,128)} %amp_map_hbm.1, bf16[64,2048]{1,0:T(8,128)(2,1)} %int_hbm.1, s32[1,32]{1,0:T(1,128)} %int_map_hbm.1, s32[2,128]{1,0:T(2,128)} %bitcast.5, f32[128]{0:T(128)} %occ_hbm.1, f32[2048]{0:T(1024)} %ve_hbm.1, f32[1,2048]{1,0:T(1,128)} %bitcast.4), custom_call_target="tpu_custom_call" | custom-call | flops 4294967296 | bytes 8388608 | tf_op jit(solution)/shard_map/pallas_call | solution.py:492
  208.6 3.1 %copy.9 = bf16[128,64,128]{2,1,0:T(8,128)(2,1)} copy(bf16[128,64,128]{2,1,0:T(8,128)(2,1)} %shard_map.73) | data formatting | bytes 4194304

commit v11 on v9

--- a/solution.py
+++ b/solution.py
@@ -463,6 +463,27 @@
     drain(out_ref.at[pl.ds(0, (NJ - 1) * pairs)], c_recv)
 
 
+def copy_out(src_ref, dst_ref, held, in_sems, out_sems):
+    parts = in_sems.shape[0]
+    size = held.shape[0] // parts
+    slices = [pl.ds(i * size, size) for i in range(parts)]
+    loads = [
+        pltpu.make_async_copy(src_ref.at[part], held.at[part], in_sems.at[i])
+        for i, part in enumerate(slices)
+    ]
+    stores = [
+        pltpu.make_async_copy(held.at[part], dst_ref.at[part], out_sems.at[i])
+        for i, part in enumerate(slices)
+    ]
+    for load in loads:
+        load.start()
+    for load, store in zip(loads, stores):
+        load.wait()
+        store.start()
+    for store in stores:
+        store.wait()
+
+
 def body(
     amplitudes, amplitude_map, integrals, integral_map, pair_list, occupied_energy, virtual_energy
 ):
@@ -471,7 +492,7 @@
     hbm = pl.BlockSpec(memory_space=pl.ANY)
     dma = pltpu.SemaphoreType.DMA
     block = pltpu.VMEM((CHUNKS, NJ, q, rows, cols), jnp.bfloat16)
-    return pl.pallas_call(
+    update = pl.pallas_call(
         kernel,
         out_shape=jax.ShapeDtypeStruct(amplitudes.shape, jnp.bfloat16),
         in_specs=[hbm] * 8,
@@ -529,6 +550,14 @@
         virtual_energy,
         virtual_energy.reshape(1, -1),
     )
+    return pl.pallas_call(
+        copy_out,
+        out_shape=jax.ShapeDtypeStruct(amplitudes.shape, jnp.bfloat16),
+        in_specs=[hbm],
+        out_specs=hbm,
+        scratch_shapes=[pltpu.VMEM(amplitudes.shape, jnp.bfloat16), dma((8,)), dma((8,))],
+        compiler_params=pltpu.CompilerParams(vmem_limit_bytes=60 * 1024 * 1024),
+    )(update)
 
 
 def solution(mesh):

time: 211 us -> 210 us (level)
  local copies, waits for them, and re-layouts: 3.08 us -> 0 us
  Pallas kernels: 207 us -> 210 us
    unnamed x1 -> x0, local copies, waits for them, and re-layouts: 3.08 us -> none
    pallas_call x0 -> x1, Pallas kernels: none -> 2.39 us  [body(): pl.pallas_call(copy_out, out_shape=jax.ShapeDtypeStruct(amplitudes.shape,...]
where the time goes in v11:
time: 210 us
  Pallas kernels  210 us (100%)
    pallas_call x1, Pallas kernels, body(): pl.pallas_call(kernel, out_shape=jax.ShapeDtypeStruct(amplitudes.shape, j...  207 us

profile of v11, /device:TPU:1, one launch (start us, length us, event | category | flops | bytes accessed | tf_op | source)
XLA Modules:
  0.0 209.7 jit_solution(145291309474958709)
XLA Ops:
  0.0 207.3 %shard_map.73.src_ref = bf16[128,64,128]{2,1,0:T(8,128)(2,1)} custom-call(bf16[8,16,64,128]{3,2,1,0:T(8,128)(2,1)} %bitcast.3, s32[1,2]{1,0:T(1,128)} %amp_map_hbm.1, bf16[64,2048]{1,0:T(8,128)(2,1)} %int_hbm.1, s32[1,32]{1,0:T(1,128)} %int_map_hbm.1, s32[2,128]{1,0:T(2,128)} %bitcast.5, f32[128]{0:T(128)} %occ_hbm.1, f32[2048]{0:T(1024)} %ve_hbm.1, ...), custom_call_target="tpu_custom_call" | custom-call | flops 4294967296 | bytes 8388608 | tf_op jit(solution)/shard_map/pallas_call | solution.py:495
  207.3 2.4 %shard_map.74 = bf16[128,64,128]{2,1,0:T(8,128)(2,1)} custom-call(bf16[128,64,128]{2,1,0:T(8,128)(2,1)} %shard_map.73.src_ref), custom_call_target="tpu_custom_call" | custom-call | tf_op jit(solution)/shard_map/pallas_call | solution.py:553

commit v12 on v11

--- a/solution.py
+++ b/solution.py
@@ -9,7 +9,7 @@
 TILE = 64
 NX, NZ, NZL, NJ, NY, NC = 4, 16, 8, 8, 4, 2
 CHUNKS = 16
-HEAD, AHEAD = 2, 4
+HEAD, AHEAD = 4, 6
 GROUP = 4
 LEGS = (5, 3)
 

time: 210 us -> 210 us (level)
  no operation moved by 1% of the time
where the time goes in v12:
time: 210 us
  Pallas kernels  210 us (100%)
    pallas_call x1, Pallas kernels, body(): pl.pallas_call(kernel, out_shape=jax.ShapeDtypeStruct(amplitudes.shape, j...  208 us

profile of v12, /device:TPU:1, one launch (start us, length us, event | category | flops | bytes accessed | tf_op | source)
XLA Modules:
  0.0 210.1 jit_solution(10665032504517287660)
XLA Ops:
  0.0 207.7 %shard_map.73.src_ref = bf16[128,64,128]{2,1,0:T(8,128)(2,1)} custom-call(bf16[8,16,64,128]{3,2,1,0:T(8,128)(2,1)} %bitcast.3, s32[1,2]{1,0:T(1,128)} %amp_map_hbm.1, bf16[64,2048]{1,0:T(8,128)(2,1)} %int_hbm.1, s32[1,32]{1,0:T(1,128)} %int_map_hbm.1, s32[2,128]{1,0:T(2,128)} %bitcast.5, f32[128]{0:T(128)} %occ_hbm.1, f32[2048]{0:T(1024)} %ve_hbm.1, ...), custom_call_target="tpu_custom_call" | custom-call | flops 4294967296 | bytes 8388608 | tf_op jit(solution)/shard_map/pallas_call | solution.py:495
  207.7 2.4 %shard_map.74 = bf16[128,64,128]{2,1,0:T(8,128)(2,1)} custom-call(bf16[128,64,128]{2,1,0:T(8,128)(2,1)} %shard_map.73.src_ref), custom_call_target="tpu_custom_call" | custom-call | tf_op jit(solution)/shard_map/pallas_call | solution.py:553
